TPU v7x, 32 devices: a whole 2x2x4 slice. The times are simulated.
32 devices in a mesh: gx: 4 (over z), gy: 8 (over y, x, core).
Axes of the slice: x: 2, y: 2, z: 4, core: 2. Of those that a mesh axis runs over, the one named last changes fastest.
Arguments:
- inputs: bfloat16 [8192, 1024], P(('gx', 'gy')), may hold values from -6 to 6
- first_weight: bfloat16 [1024, 1024], replicated, may hold values from -0.1875 to 0.1875
- second_weight: bfloat16 [1024, 512], replicated, may hold values from -0.1875 to 0.1875
- targets: bfloat16 [8192], P(('gx', 'gy')), may hold values from -6 to 6
- noise_var: float32 [32], P(('gx', 'gy')), may hold values from 0.5 to 4
- assignment: int32 [8192, 1], P(('gx', 'gy')), may hold values from 0 to 31; in each aligned block of 256 rows (0 to 255, 256 to 511, ...) at most 16 rows name the same one
Outputs:
- grad_first: float32 [1024, 1024], P(('gx', 'gy'))
- grad_second: float32 [1024, 512], P(('gx', 'gy'))
- expert_loss: float32 [32], P(('gx', 'gy'))
Inputs may be any that keep to these rules, and one draw needn't show every extreme that they name: `assignment`: the rows of one device name one expert at most 16 times; every expert is named by some row.
All inputs are finite; a program needn't handle non-finite values.
Results may differ from a plain program's by a relative error of at most 0.0033.
Values may be sent and summed in bfloat16 or wider, within the bound.
No kernel may reach another device: no remote copies, remote signals or barrier semaphores. Data moves between devices by JAX's collectives and lax.ppermute only.
A program may use at most 64 MiB of HBM per device.

v0:
```python
import functools

import jax
import jax.numpy as jnp
from jax import lax
from jax.experimental import pallas as pl
from jax.experimental.pallas import tpu as pltpu
from jax.sharding import PartitionSpec as P

CAP = 512
POWERS = 16
BF16 = jnp.bfloat16
F32 = jnp.float32
EXACT = lax.Precision.HIGHEST
VMEM = pl.BlockSpec(memory_space=pltpu.VMEM)
SMEM = pl.BlockSpec(memory_space=pltpu.SMEM)
PARAMS = pltpu.CompilerParams(vmem_limit_bytes=48 * 1024 * 1024)


def dot(left, right, left_dim=1, right_dim=0, precision=None):
    return lax.dot_general(
        left,
        right,
        (((left_dim,), (right_dim,)), ((), ())),
        preferred_element_type=F32,
        precision=precision,
    )


def iota(shape, dim):
    return lax.broadcasted_iota(jnp.int32, shape, dim)


def dispatch_kernel(devices, assign_ref, targ_ref, rows_ref, out_ref):
    assign = assign_ref[...]
    count, width = rows_ref.shape
    per_slot = CAP // devices
    onehot = iota((devices, count), 0) == assign
    earlier = (iota((count, count), 0) < iota((count, count), 1)).astype(BF16)
    rank = dot(onehot.astype(BF16), earlier)
    slot = jnp.sum(jnp.where(onehot, rank, 0.0), axis=0, keepdims=True)
    place = assign * per_slot + slot.astype(jnp.int32)
    here = iota((CAP, count), 0) == place
    out_ref[:, :width] = dot(here.astype(BF16), rows_ref[...]).astype(BF16)
    targ = jnp.sum(jnp.where(here, targ_ref[...].astype(F32), 0.0), axis=1, keepdims=True)
    out_ref[:, width:] = jnp.broadcast_to(targ, (CAP, 128)).astype(BF16)


def gram_rows_to_column(gram, row):
    parts = []
    for start in range(0, CAP, 64):
        product = gram[start : start + 64, :] * row
        folded = sum(product[:, lane : lane + 128] for lane in range(0, CAP, 128))
        parts.append(jnp.sum(folded, axis=1, keepdims=True))
    return jnp.concatenate(parts, axis=0)


def gram_column_to_row(gram, column):
    total = jnp.zeros((8, CAP), F32)
    for start in range(0, CAP, 64):
        product = gram[start : start + 64, :] * column[start : start + 64, :]
        total = total + jnp.sum(product.reshape(8, 8, CAP), axis=0)
    return jnp.sum(total, axis=0, keepdims=True)


def expert_kernel(
    blocks,
    parity_ref,
    noise_ref,
    got_ref,
    first_ref,
    second_ref,
    keep1_ref,
    send1_ref,
    keep2_ref,
    send2_ref,
    loss_ref,
    pre_ref,
    hid_ref,
    feat_ref,
    gram_ref,
    grad_ref,
    pgrad_ref,
    xt_ref,
    ht_ref,
):
    din, hid = first_ref.shape
    feat = second_ref.shape[1]
    step = 128
    chunks = CAP // step

    def split_parity(source, target):
        turned = source.T.reshape(blocks // 2, 2, din // blocks, CAP)
        target[0] = turned[:, 0].reshape(din // 2, CAP)
        target[1] = turned[:, 1].reshape(din // 2, CAP)

    @pl.loop(0, chunks)
    def _(i):
        rows = pl.ds(pl.multiple_of(i * step, step), step)
        pre = dot(got_ref[rows, :din], first_ref[...])
        pre_ref[rows, :] = pre
        hidden = (pre * jax.nn.sigmoid(pre)).astype(BF16)
        hid_ref[rows, :] = hidden
        feat_ref[rows, :] = dot(hidden, second_ref[...]).astype(BF16)

    split_parity(got_ref[:, :din], xt_ref)
    split_parity(hid_ref[...], ht_ref)

    feats = feat_ref[...]
    gram_ref[...] = dot(feats, feats, 1, 1) * (1.0 / feat)
    gram = gram_ref[...]
    noise = noise_ref[0]
    squares = sum(
        jnp.sum((gram[i : i + 64, :] * gram[i : i + 64, :]).reshape(8, 8, CAP), axis=0)
        for i in range(0, CAP, 64)
    )
    root = jnp.sqrt(jnp.sum(squares, keepdims=True) + 1e-06)
    theta = root + noise
    inverse = 1.0 / theta
    shrink = root * inverse

    targ = got_ref[:, din:].astype(F32)
    column = targ[:, :1]
    lane = iota((CAP, 128), 1)
    sub = iota((POWERS, CAP), 0)
    columns = jnp.where(lane == 0, targ, 0.0)
    row_set = jnp.zeros((POWERS, CAP), F32)
    targ_row = targ.T[:1, :]
    row = None
    previous_row = targ_row
    for k in range(1, POWERS - 1):
        if k % 2 == 1:
            before = previous_row if k == 1 else columns.T[k - 1 : k, :]
            row = shrink * before - gram_column_to_row(gram, column) * inverse
            row_set = row_set + jnp.where(sub == k, row, 0.0)
        else:
            before = row.T
            column = shrink * before - gram_rows_to_column(gram, row) * inverse
            columns = columns + jnp.where(lane == k, column, 0.0)
    powers = row_set + columns.T[:POWERS, :]
    moments = jnp.sum(powers * targ_row, axis=1, keepdims=True)
    last = jnp.sum(powers[7:8, :] * powers[8:9, :], axis=1, keepdims=True)
    loss_ref[...] = 0.5 * inverse * (jnp.sum(moments, axis=0, keepdims=True) + last)
    mask = (iota((POWERS, POWERS), 0) + iota((POWERS, POWERS), 1) <= POWERS - 2).astype(F32)
    sums = dot(mask, powers, precision=EXACT)
    outer = dot(powers, sums, 0, 0, precision=EXACT) + (16.0 * last / root) * gram
    high = outer.astype(BF16)
    low = (outer - high.astype(F32)).astype(BF16)
    scale = -inverse * inverse * (1.0 / feat)
    grad_ref[...] = ((dot(high, feats) + dot(low, feats)) * scale).astype(BF16)

    parity = parity_ref[0]
    keep2_ref[...] = dot(ht_ref[parity], grad_ref[...])
    send2_ref[...] = dot(ht_ref[1 - parity], grad_ref[...])

    @pl.loop(0, chunks)
    def _(i):
        rows = pl.ds(pl.multiple_of(i * step, step), step)
        hidden_grad = dot(grad_ref[rows, :], second_ref[...], 1, 1)
        pre = pre_ref[rows, :]
        sigma = jax.nn.sigmoid(pre)
        pgrad_ref[rows, :] = (hidden_grad * sigma * (1.0 + pre * (1.0 - sigma))).astype(BF16)

    keep1_ref[...] = dot(xt_ref[parity], pgrad_ref[...])
    send1_ref[...] = dot(xt_ref[1 - parity], pgrad_ref[...])


def split_kernel(group, count, place_ref, *refs):
    arrays, outs = refs[: -2 * group], refs[-2 * group :]
    place = place_ref[0]
    for which in range(2):
        parts = arrays[which * count : (which + 1) * count]
        for d in range(group):
            target = jnp.bitwise_xor(place, d)
            out = outs[which * group + d]
            total = parts[0][:, target].astype(F32)
            for part in parts[1:]:
                total = total + part[:, target].astype(F32)
            out[...] = total.astype(out.dtype)


def split_stage(place, first_parts, second_parts, group):
    def shapes(part):
        shape = (part.shape[0], *part.shape[2:])
        return [jax.ShapeDtypeStruct(shape, F32 if d == 0 else BF16) for d in range(group)]

    outs = shapes(first_parts[0]) + shapes(second_parts[0])
    made = pl.pallas_call(
        functools.partial(split_kernel, group, len(first_parts)),
        out_shape=outs,
        in_specs=[SMEM] + [VMEM] * (2 * len(first_parts)),
        out_specs=[VMEM] * (2 * group),
        compiler_params=PARAMS,
    )(place, *first_parts, *second_parts)
    return made[:group], made[group:]


def swap(array, axis, distance):
    count = lax.axis_size(axis)
    return lax.ppermute(array, axis, [(i, i ^ distance) for i in range(count)])


def exchange(parts, axis, unit):
    return [parts[0]] + [swap(parts[d], axis, d * unit) for d in range(1, len(parts))]


def on_device(inputs, first_weight, second_weight, targets, noise_var, assignment):
    gx_count = lax.axis_size("gx")
    gy_count = lax.axis_size("gy")
    devices = gx_count * gy_count
    per_slot = CAP // devices
    rows, din = inputs.shape
    hid, feat = second_weight.shape
    own_rows = din // devices
    gx = lax.axis_index("gx")
    gy = lax.axis_index("gy")

    def scalar(x):
        return x.astype(jnp.int32).reshape(1)

    sent = pl.pallas_call(
        functools.partial(dispatch_kernel, devices),
        out_shape=jax.ShapeDtypeStruct((CAP, din + 128), BF16),
        in_specs=[VMEM] * 3,
        out_specs=VMEM,
        compiler_params=PARAMS,
    )(assignment.reshape(1, rows), targets.reshape(1, rows), inputs)
    got = lax.all_to_all(
        sent.reshape(devices, per_slot, din + 128),
        ("gx", "gy"),
        split_axis=0,
        concat_axis=0,
        tiled=True,
    ).reshape(CAP, din + 128)

    half = din // 2
    keep1, send1, keep2, send2, loss = pl.pallas_call(
        functools.partial(expert_kernel, devices),
        out_shape=[
            jax.ShapeDtypeStruct((half, hid), F32),
            jax.ShapeDtypeStruct((half, hid), F32),
            jax.ShapeDtypeStruct((half, feat), F32),
            jax.ShapeDtypeStruct((half, feat), F32),
            jax.ShapeDtypeStruct((1, 1), F32),
        ],
        in_specs=[SMEM, SMEM, VMEM, VMEM, VMEM],
        out_specs=[VMEM] * 5,
        scratch_shapes=[
            pltpu.VMEM((CAP, hid), F32),
            pltpu.VMEM((CAP, hid), BF16),
            pltpu.VMEM((CAP, feat), BF16),
            pltpu.VMEM((CAP, CAP), F32),
            pltpu.VMEM((CAP, feat), BF16),
            pltpu.VMEM((CAP, hid), BF16),
            pltpu.VMEM((2, half, CAP), BF16),
            pltpu.VMEM((2, half, CAP), BF16),
        ],
        compiler_params=PARAMS,
    )(scalar(gy % 2), noise_var, got, first_weight, second_weight)

    plane = gy_count // 2
    got2 = swap(send2, "gy", 1)
    got1 = swap(send1, "gy", 1)

    def cut(array, outer, group):
        return array.reshape(outer, group, own_rows, array.shape[-1])

    first_parts, second_parts = split_stage(
        scalar(gy // 2),
        [cut(a, gx_count, plane) for a in (keep1, got1)],
        [cut(a, gx_count, plane) for a in (keep2, got2)],
        plane,
    )
    second_parts = exchange(second_parts, "gy", 2)
    first_parts = exchange(first_parts, "gy", 2)
    first_parts, second_parts = split_stage(
        scalar(gx),
        [cut(a, 1, gx_count) for a in first_parts],
        [cut(a, 1, gx_count) for a in second_parts],
        gx_count,
    )
    second_parts = exchange(second_parts, "gx", 1)
    first_parts = exchange(first_parts, "gx", 1)
    first_total = sum(a.astype(F32) for a in first_parts)
    second_total = sum(a.astype(F32) for a in second_parts)
    return (
        first_total.reshape(own_rows, hid),
        second_total.reshape(own_rows, feat),
        loss.reshape(1),
    )


def solution(mesh):
    return jax.shard_map(
        on_device,
        mesh=mesh,
        in_specs=(
            P(("gx", "gy"), None),
            P(),
            P(),
            P(("gx", "gy")),
            P(("gx", "gy")),
            P(("gx", "gy"), None),
        ),
        out_specs=(P(("gx", "gy"), None), P(("gx", "gy"), None), P(("gx", "gy"))),
        check_vma=False,
    )
```

profile of v0, /device:TPU:0, one launch (start us, length us, event | category | flops | bytes accessed | tf_op | source)
XLA Modules:
  0.0 100.8 jit_solution(9895485338463242527)
XLA Ops:
  0.6 0.0 copy-start.1
  0.6 0.7 reshape.76.targ_ref
  1.4 0.0 copy-start.2
  1.4 1.0 %copy-done.2 = bf16[256,1024]{1,0:T(8,128)(2,1)S(1)} copy-done((bf16[256,1024]{1,0:T(8,128)(2,1)S(1)}, bf16[256,1024]{1,0:T(8,128)(2,1)}, u32[]{:S(2)}) %copy-start.2) | copy-done | bytes 524312
  2.4 0.0 copy-start.3
  2.4 0.7 copy-done.3
  3.1 1.7 %shard_map.85 = bf16[512,1152]{1,0:T(8,128)(2,1)} custom-call(s32[1,256]{1,0:T(1,128)S(1)} %bitcast.35, bf16[1,256]{1,0:T(2,128)(2,1)S(1)} %reshape.76.targ_ref, bf16[256,1024]{1,0:T(8,128)(2,1)S(1)} %copy-done.2), custom_call_target="tpu_custom_call" | custom-call | tf_op jit(solution)/shard_map/pallas_call | solution.py:221
  4.8 7.3 %all-to-all-start = ((bf16[32,16,1152]{2,1,0:T(8,128)(2,1)}), bf16[32,16,1152]{2,1,0:T(8,128)(2,1)S(1)}, u32[]{:S(2)}, u32[]{:S(2)}) async-start(bf16[32,16,1152]{2,1,0:T(8,128)(2,1)} %bitcast.4), calls=%async_computation | async-start | bytes 2359296 | tf_op jit(solution)/shard_map/all_to_all | solution.py:228
  12.8 28.4 %all-to-all-done = bf16[32,16,1152]{2,1,0:T(8,128)(2,1)S(1)} async-done(((bf16[32,16,1152]{2,1,0:T(8,128)(2,1)}), bf16[32,16,1152]{2,1,0:T(8,128)(2,1)S(1)}, u32[]{:S(2)}, u32[]{:S(2)}) %all-to-all-start) | async-done | bytes 1179680 | tf_op jit(solution)/shard_map/all_to_all | solution.py:228
  41.2 0.0 copy-done.1
  41.2 15.0 %shard_map.86 = (f32[512,1024]{1,0:T(8,128)}, f32[512,1024]{1,0:T(8,128)}, f32[512,512]{1,0:T(8,128)S(1)}, f32[512,512]{1,0:T(8,128)}, f32[1,1]{1,0:T(1,128)}) custom-call(s32[1]{0:T(128)} %bitcast.2.parity_ref, f32[1]{0:T(128)S(6)} %copy.9.noise_ref, bf16[512,1152]{1,0:T(8,128)(2,1)S(1)} %bitcast.23, bf16[1024,1024]{1,0:T(8,128)(2,1)} %first_ref.1, ...), custom_call_target="tpu_custom_call" | custom-call | tf_op jit(solution)/shard_map/pallas_call | solution.py:237
  56.2 0.0 collective-permute-start
  56.2 0.5 collective-permute-start.1
  56.7 5.0 %collective-permute-done.1 = f32[512,512]{1,0:T(8,128)S(1)} collective-permute-done((f32[512,512]{1,0:T(8,128)}, f32[512,512]{1,0:T(8,128)S(1)}, u32[]{:S(2)}, u32[]{:S(2)}) %collective-permute-start.1) | collective-permute-done | bytes 1048608 | tf_op jit(solution)/shard_map/ppermute | solution.py:200
  61.7 0.5 collective-permute-done
  62.2 0.0 copy-start
  62.2 1.6 %copy-done = f32[512,1024]{1,0:T(8,128)S(1)} copy-done((f32[512,1024]{1,0:T(8,128)S(1)}, f32[512,1024]{1,0:T(8,128)}, u32[]{:S(2)}) %copy-start) | copy-done | bytes 2097176
  63.7 2.6 %shard_map.87 = (f32[4,32,1024]{2,1,0:T(8,128)S(1)}, bf16[4,32,1024]{2,1,0:T(8,128)(2,1)}, bf16[4,32,1024]{2,1,0:T(8,128)(2,1)S(1)}, bf16[4,32,1024]{2,1,0:T(8,1...) custom-call(s32[1]{0:T(128)} %bitcast.1.place_ref, ...), custom_call_target="tpu_custom_call" | custom-call | tf_op jit(solution)/shard_map/pallas_call | solution.py:188
  66.4 1.4 %collective-permute-start.5 = (bf16[4,32,512]{2,1,0:T(8,128)(2,1)S(1)}, bf16[4,32,512]{2,1,0:T(8,128)(2,1)S(1)}, u32[]{:S(2)}, u32[]{:S(2)}) collective-permute-start(bf16[4,32,512]{2,1,0:T(8,128)(2,1)S(1)} %get-tuple-element.33), channel_id=1, source_target_pairs={{0,2},{1,3},{2,0},{3,1},{4,6},{5,7},{6,4},{7,5},{8,10},{9,11},{10,... | collective-permute-start | bytes 393224 | tf_op jit(solution)/shard_map/ppermute | solution.py:200
  67.8 0.6 collective-permute-start.2
  68.4 1.4 %collective-permute-start.3 = (bf16[4,32,1024]{2,1,0:T(8,128)(2,1)S(1)}, bf16[4,32,1024]{2,1,0:T(8,128)(2,1)S(1)}, u32[]{:S(2)}, u32[]{:S(2)}) collective-permute-start(bf16[4,32,1024]{2,1,0:T(8,128)(2,1)S(1)} %get-tuple-element.30), channel_id=1, source_target_pairs={{0,4},{1,5},{2,6},{3,7},{4,0},{5,1},{6,2},{7,3},{8,12},{9,13},{10,... | collective-permute-start | bytes 786440 | tf_op jit(solution)/shard_map/ppermute | solution.py:200
  69.8 1.5 %collective-permute-start.4 = (bf16[4,32,1024]{2,1,0:T(8,128)(2,1)S(1)}, bf16[4,32,1024]{2,1,0:T(8,128)(2,1)S(1)}, u32[]{:S(2)}, u32[]{:S(2)}) collective-permute-start(bf16[4,32,1024]{2,1,0:T(8,128)(2,1)S(1)} %get-tuple-element.31), channel_id=1, source_target_pairs={{0,6},{1,7},{2,4},{3,5},{4,2},{5,3},{6,0},{7,1},{8,14},{9,15},{10,... | collective-permute-start | bytes 786440 | tf_op jit(solution)/shard_map/ppermute | solution.py:200
  71.3 1.5 %collective-permute-start.6 = (bf16[4,32,512]{2,1,0:T(8,128)(2,1)}, bf16[4,32,512]{2,1,0:T(8,128)(2,1)S(1)}, u32[]{:S(2)}, u32[]{:S(2)}) collective-permute-start(bf16[4,32,512]{2,1,0:T(8,128)(2,1)} %get-tuple-element.34), channel_id=1, source_target_pairs={{0,4},{1,5},{2,6},{3,7},{4,0},{5,1},{6,2},{7,3},{8,12},{9,13},{10,... | collective-permute-start | bytes 393224 | tf_op jit(solution)/shard_map/ppermute | solution.py:200
  72.8 0.0 collective-permute-done.5
  72.8 2.3 %collective-permute-start.7 = (bf16[4,32,512]{2,1,0:T(8,128)(2,1)}, bf16[4,32,512]{2,1,0:T(8,128)(2,1)S(1)}, u32[]{:S(2)}, u32[]{:S(2)}) collective-permute-start(bf16[4,32,512]{2,1,0:T(8,128)(2,1)} %get-tuple-element.35), channel_id=1, source_target_pairs={{0,6},{1,7},{2,4},{3,5},{4,2},{5,3},{6,0},{7,1},{8,14},{9,15},{10,... | collective-permute-start | bytes 393224 | tf_op jit(solution)/shard_map/ppermute | solution.py:200
  75.1 12.4 %collective-permute-done.6 = bf16[4,32,512]{2,1,0:T(8,128)(2,1)S(1)} collective-permute-done((bf16[4,32,512]{2,1,0:T(8,128)(2,1)}, bf16[4,32,512]{2,1,0:T(8,128)(2,1)S(1)}, u32[]{:S(2)}, u32[]{:S(2)}) %collective-permute-start.6) | collective-permute-done | bytes 131104 | tf_op jit(solution)/shard_map/ppermute | solution.py:200
  87.4 0.0 collective-permute-done.7
  87.4 0.0 collective-permute-done.2
  87.4 0.0 collective-permute-done.3
  87.4 0.0 collective-permute-done.4
  87.4 0.2 shard_map.88
  87.6 0.8 collective-permute-start.11
  88.4 1.1 %collective-permute-start.12 = (bf16[1,32,512]{2,1,0:T(8,128)(2,1)S(1)}, bf16[1,32,512]{2,1,0:T(8,128)(2,1)S(1)}, u32[]{:S(2)}, u32[]{:S(2)}) collective-permute-start(bf16[1,32,512]{2,1,0:T(8,128)(2,1)S(1)} %get-tuple-element.42), channel_id=1, source_target_pairs={{0,16},{8,24},{16,0},{24,8},{1,17},{9,25},{17,1},{25,9},{2,18},{10... | collective-permute-start | bytes 98312 | tf_op jit(solution)/shard_map/ppermute | solution.py:200
  89.5 2.6 %collective-permute-start.13 = (bf16[1,32,512]{2,1,0:T(8,128)(2,1)S(1)}, bf16[1,32,512]{2,1,0:T(8,128)(2,1)S(1)}, u32[]{:S(2)}, u32[]{:S(2)}) collective-permute-start(bf16[1,32,512]{2,1,0:T(8,128)(2,1)S(1)} %get-tuple-element.43), channel_id=1, source_target_pairs={{0,24},{8,16},{16,8},{24,0},{1,25},{9,17},{17,9},{25,1},{2,26},{10... | collective-permute-start | bytes 98312 | tf_op jit(solution)/shard_map/ppermute | solution.py:200
  92.1 0.0 collective-permute-start.8
  92.1 1.8 %collective-permute-start.9 = (bf16[1,32,1024]{2,1,0:T(8,128)(2,1)S(1)}, bf16[1,32,1024]{2,1,0:T(8,128)(2,1)S(1)}, u32[]{:S(2)}, u32[]{:S(2)}) collective-permute-start(bf16[1,32,1024]{2,1,0:T(8,128)(2,1)S(1)} %get-tuple-element.38), channel_id=1, source_target_pairs={{0,16},{8,24},{16,0},{24,8},{1,17},{9,25},{17,1},{25,9},{2,18},{10... | collective-permute-start | bytes 196616 | tf_op jit(solution)/shard_map/ppermute | solution.py:200
  93.9 0.0 collective-permute-done.11
  93.9 2.6 %collective-permute-start.10 = (bf16[1,32,1024]{2,1,0:T(8,128)(2,1)S(1)}, bf16[1,32,1024]{2,1,0:T(8,128)(2,1)S(1)}, u32[]{:S(2)}, u32[]{:S(2)}) collective-permute-start(bf16[1,32,1024]{2,1,0:T(8,128)(2,1)S(1)} %get-tuple-element.39), channel_id=1, source_target_pairs={{0,24},{8,16},{16,8},{24,0},{1,25},{9,17},{17,9},{25,1},{2,26},{10... | collective-permute-start | bytes 196616 | tf_op jit(solution)/shard_map/ppermute | solution.py:200
  96.5 0.0 collective-permute-done.12
  96.5 0.0 collective-permute-done.13
  96.5 0.7 add_bitcast_fusion.1
  97.1 0.3 collective-permute-done.8
  97.4 0.7 collective-permute-done.9
  98.1 2.0 %collective-permute-done.10 = bf16[1,32,1024]{2,1,0:T(8,128)(2,1)S(1)} collective-permute-done((bf16[1,32,1024]{2,1,0:T(8,128)(2,1)S(1)}, bf16[1,32,1024]{2,1,0:T(8,128)(2,1)S(1)}, u32[]{:S(2)}, u32[]{:S(2)}) %collective-permute-start.10) | collective-permute-done | bytes 65568 | tf_op jit(solution)/shard_map/ppermute | solution.py:200
  100.1 0.7 add_bitcast_fusion
Async XLA Ops:
  0.6 40.6 %copy-start.1 = (bf16[1024,512]{1,0:T(8,128)(2,1)S(1)}, bf16[1024,512]{1,0:T(8,128)(2,1)}, u32[]{:S(2)}) copy-start(bf16[1024,512]{1,0:T(8,128)(2,1)} %second_ref.1) | copy-start | bytes 3145732
  1.4 1.0 %copy-start.2 = (bf16[256,1024]{1,0:T(8,128)(2,1)S(1)}, bf16[256,1024]{1,0:T(8,128)(2,1)}, u32[]{:S(2)}) copy-start(bf16[256,1024]{1,0:T(8,128)(2,1)} %rows_ref.1) | copy-start | bytes 1572868
  2.4 0.7 copy-start.3
  4.8 36.4 %all-to-all-start = ((bf16[32,16,1152]{2,1,0:T(8,128)(2,1)}), bf16[32,16,1152]{2,1,0:T(8,128)(2,1)S(1)}, u32[]{:S(2)}, u32[]{:S(2)}) async-start(bf16[32,16,1152]{2,1,0:T(8,128)(2,1)} %bitcast.4), calls=%async_computation | async-start | bytes 2359296 | tf_op jit(solution)/shard_map/all_to_all | solution.py:228
  56.2 6.0 %collective-permute-start = (f32[512,1024]{1,0:T(8,128)}, f32[512,1024]{1,0:T(8,128)}, u32[]{:S(2)}, u32[]{:S(2)}) collective-permute-start(f32[512,1024]{1,0:T(8,128)} %get-tuple-element.25), channel_id=1, source_target_pairs={{0,1},{1,0},{2,3},{3,2},{4,5},{5,4},{6,7},{7,6},{8,9},{9,8},{10,11... | collective-permute-start | bytes 6291464 | tf_op jit(solution)/shard_map/ppermute | solution.py:200
  56.2 5.5 %collective-permute-start.1 = (f32[512,512]{1,0:T(8,128)}, f32[512,512]{1,0:T(8,128)S(1)}, u32[]{:S(2)}, u32[]{:S(2)}) collective-permute-start(f32[512,512]{1,0:T(8,128)} %get-tuple-element.27), channel_id=1, source_target_pairs={{0,1},{1,0},{2,3},{3,2},{4,5},{5,4},{6,7},{7,6},{8,9},{9,8},{10,11... | collective-permute-start | bytes 3145736 | tf_op jit(solution)/shard_map/ppermute | solution.py:200
  62.2 1.6 %copy-start = (f32[512,1024]{1,0:T(8,128)S(1)}, f32[512,1024]{1,0:T(8,128)}, u32[]{:S(2)}) copy-start(f32[512,1024]{1,0:T(8,128)} %get-tuple-element.24) | copy-start | bytes 6291460
  66.4 6.4 %collective-permute-start.5 = (bf16[4,32,512]{2,1,0:T(8,128)(2,1)S(1)}, bf16[4,32,512]{2,1,0:T(8,128)(2,1)S(1)}, u32[]{:S(2)}, u32[]{:S(2)}) collective-permute-start(bf16[4,32,512]{2,1,0:T(8,128)(2,1)S(1)} %get-tuple-element.33), channel_id=1, source_target_pairs={{0,2},{1,3},{2,0},{3,1},{4,6},{5,7},{6,4},{7,5},{8,10},{9,11},{10,... | collective-permute-start | bytes 393224 | tf_op jit(solution)/shard_map/ppermute | solution.py:200
  67.8 19.6 %collective-permute-start.2 = (bf16[4,32,1024]{2,1,0:T(8,128)(2,1)}, bf16[4,32,1024]{2,1,0:T(8,128)(2,1)S(1)}, u32[]{:S(2)}, u32[]{:S(2)}) collective-permute-start(bf16[4,32,1024]{2,1,0:T(8,128)(2,1)} %get-tuple-element.29), channel_id=1, source_target_pairs={{0,2},{1,3},{2,0},{3,1},{4,6},{5,7},{6,4},{7,5},{8,10},{9,11},{10,... | collective-permute-start | bytes 786440 | tf_op jit(solution)/shard_map/ppermute | solution.py:200
  68.4 19.0 %collective-permute-start.3 = (bf16[4,32,1024]{2,1,0:T(8,128)(2,1)S(1)}, bf16[4,32,1024]{2,1,0:T(8,128)(2,1)S(1)}, u32[]{:S(2)}, u32[]{:S(2)}) collective-permute-start(bf16[4,32,1024]{2,1,0:T(8,128)(2,1)S(1)} %get-tuple-element.30), channel_id=1, source_target_pairs={{0,4},{1,5},{2,6},{3,7},{4,0},{5,1},{6,2},{7,3},{8,12},{9,13},{10,... | collective-permute-start | bytes 786440 | tf_op jit(solution)/shard_map/ppermute | solution.py:200
  69.8 17.6 %collective-permute-start.4 = (bf16[4,32,1024]{2,1,0:T(8,128)(2,1)S(1)}, bf16[4,32,1024]{2,1,0:T(8,128)(2,1)S(1)}, u32[]{:S(2)}, u32[]{:S(2)}) collective-permute-start(bf16[4,32,1024]{2,1,0:T(8,128)(2,1)S(1)} %get-tuple-element.31), channel_id=1, source_target_pairs={{0,6},{1,7},{2,4},{3,5},{4,2},{5,3},{6,0},{7,1},{8,14},{9,15},{10,... | collective-permute-start | bytes 786440 | tf_op jit(solution)/shard_map/ppermute | solution.py:200
  71.3 16.1 %collective-permute-start.6 = (bf16[4,32,512]{2,1,0:T(8,128)(2,1)}, bf16[4,32,512]{2,1,0:T(8,128)(2,1)S(1)}, u32[]{:S(2)}, u32[]{:S(2)}) collective-permute-start(bf16[4,32,512]{2,1,0:T(8,128)(2,1)} %get-tuple-element.34), channel_id=1, source_target_pairs={{0,4},{1,5},{2,6},{3,7},{4,0},{5,1},{6,2},{7,3},{8,12},{9,13},{10,... | collective-permute-start | bytes 393224 | tf_op jit(solution)/shard_map/ppermute | solution.py:200
  72.8 14.6 %collective-permute-start.7 = (bf16[4,32,512]{2,1,0:T(8,128)(2,1)}, bf16[4,32,512]{2,1,0:T(8,128)(2,1)S(1)}, u32[]{:S(2)}, u32[]{:S(2)}) collective-permute-start(bf16[4,32,512]{2,1,0:T(8,128)(2,1)} %get-tuple-element.35), channel_id=1, source_target_pairs={{0,6},{1,7},{2,4},{3,5},{4,2},{5,3},{6,0},{7,1},{8,14},{9,15},{10,... | collective-permute-start | bytes 393224 | tf_op jit(solution)/shard_map/ppermute | solution.py:200
  87.6 6.3 %collective-permute-start.11 = (bf16[1,32,512]{2,1,0:T(8,128)(2,1)S(1)}, bf16[1,32,512]{2,1,0:T(8,128)(2,1)S(1)}, u32[]{:S(2)}, u32[]{:S(2)}) collective-permute-start(bf16[1,32,512]{2,1,0:T(8,128)(2,1)S(1)} %get-tuple-element.41), channel_id=1, source_target_pairs={{0,8},{8,0},{16,24},{24,16},{1,9},{9,1},{17,25},{25,17},{2,10},{10... | collective-permute-start | bytes 98312 | tf_op jit(solution)/shard_map/ppermute | solution.py:200
  88.4 8.1 %collective-permute-start.12 = (bf16[1,32,512]{2,1,0:T(8,128)(2,1)S(1)}, bf16[1,32,512]{2,1,0:T(8,128)(2,1)S(1)}, u32[]{:S(2)}, u32[]{:S(2)}) collective-permute-start(bf16[1,32,512]{2,1,0:T(8,128)(2,1)S(1)} %get-tuple-element.42), channel_id=1, source_target_pairs={{0,16},{8,24},{16,0},{24,8},{1,17},{9,25},{17,1},{25,9},{2,18},{10... | collective-permute-start | bytes 98312 | tf_op jit(solution)/shard_map/ppermute | solution.py:200
  89.5 7.0 %collective-permute-start.13 = (bf16[1,32,512]{2,1,0:T(8,128)(2,1)S(1)}, bf16[1,32,512]{2,1,0:T(8,128)(2,1)S(1)}, u32[]{:S(2)}, u32[]{:S(2)}) collective-permute-start(bf16[1,32,512]{2,1,0:T(8,128)(2,1)S(1)} %get-tuple-element.43), channel_id=1, source_target_pairs={{0,24},{8,16},{16,8},{24,0},{1,25},{9,17},{17,9},{25,1},{2,26},{10... | collective-permute-start | bytes 98312 | tf_op jit(solution)/shard_map/ppermute | solution.py:200
  92.1 5.3 %collective-permute-start.8 = (bf16[1,32,1024]{2,1,0:T(8,128)(2,1)S(1)}, bf16[1,32,1024]{2,1,0:T(8,128)(2,1)S(1)}, u32[]{:S(2)}, u32[]{:S(2)}) collective-permute-start(bf16[1,32,1024]{2,1,0:T(8,128)(2,1)S(1)} %get-tuple-element.37), channel_id=1, source_target_pairs={{0,8},{8,0},{16,24},{24,16},{1,9},{9,1},{17,25},{25,17},{2,10},{10... | collective-permute-start | bytes 196616 | tf_op jit(solution)/shard_map/ppermute | solution.py:200
  92.1 6.0 %collective-permute-start.9 = (bf16[1,32,1024]{2,1,0:T(8,128)(2,1)S(1)}, bf16[1,32,1024]{2,1,0:T(8,128)(2,1)S(1)}, u32[]{:S(2)}, u32[]{:S(2)}) collective-permute-start(bf16[1,32,1024]{2,1,0:T(8,128)(2,1)S(1)} %get-tuple-element.38), channel_id=1, source_target_pairs={{0,16},{8,24},{16,0},{24,8},{1,17},{9,25},{17,1},{25,9},{2,18},{10... | collective-permute-start | bytes 196616 | tf_op jit(solution)/shard_map/ppermute | solution.py:200
  93.9 6.2 %collective-permute-start.10 = (bf16[1,32,1024]{2,1,0:T(8,128)(2,1)S(1)}, bf16[1,32,1024]{2,1,0:T(8,128)(2,1)S(1)}, u32[]{:S(2)}, u32[]{:S(2)}) collective-permute-start(bf16[1,32,1024]{2,1,0:T(8,128)(2,1)S(1)} %get-tuple-element.39), channel_id=1, source_target_pairs={{0,24},{8,16},{16,8},{24,0},{1,25},{9,17},{17,9},{25,1},{2,26},{10... | collective-permute-start | bytes 196616 | tf_op jit(solution)/shard_map/ppermute | solution.py:200
where the time goes:
time: 101 us
  waiting for transfers between devices  49.2 us (49%)
  starting transfers between devices  25.3 us (25%)
  Pallas kernels  19.4 us (19%)
  local copies, waits for them, and re-layouts  4.06 us (4%)
  between operations  1.35 us (1%)
  other arithmetic  1.34 us (1%)
    all_to_all x1, waiting for transfers between devices, on_device(): lax.all_to_all(sent.reshape(devices, per_slot, din + 128), ('gx', 'gy'),...  28.4 us
    ppermute x14, waiting for transfers between devices, swap(): return lax.ppermute(array, axis, [(i, i ^ distance) for i in range(count)])  20.8 us
    ppermute x14, starting transfers between devices, swap(): return lax.ppermute(array, axis, [(i, i ^ distance) for i in range(count)])  18 us
    pallas_call x1, Pallas kernels, on_device(): pl.pallas_call(functools.partial(expert_kernel, devices), out_shape=[jax....  15 us
    all_to_all x1, starting transfers between devices, on_device(): lax.all_to_all(sent.reshape(devices, per_slot, din + 128), ('gx', 'gy'),...  7.3 us
    unnamed x8, local copies, waits for them, and re-layouts  3.31 us
    pallas_call x2, Pallas kernels, split_stage(): pl.pallas_call(functools.partial(split_kernel, group, len(first_parts)),...  2.8 us
  transfers between devices with their start and end apart: 15, of which 7 were waited for; matrix products, arithmetic and copies ran while one was open for 1% of the time, Pallas kernels for 0%

commit v1 on v0

v1 whole, which is shorter than its diff:
```python
import functools

import jax
import jax.numpy as jnp
from jax import lax
from jax.experimental import pallas as pl
from jax.experimental.pallas import tpu as pltpu
from jax.sharding import PartitionSpec as P

CAP = 512
POWERS = 16
BF16 = jnp.bfloat16
F32 = jnp.float32
EXACT = lax.Precision.HIGHEST
VMEM = pl.BlockSpec(memory_space=pltpu.VMEM)
SMEM = pl.BlockSpec(memory_space=pltpu.SMEM)
ANY = pl.BlockSpec(memory_space=pl.ANY)
PARAMS = pltpu.CompilerParams(vmem_limit_bytes=24 * 1024 * 1024)


def cost(work):
    return pl.CostEstimate(flops=int(work), bytes_accessed=0, transcendentals=0)


def dot(left, right, left_dim=1, right_dim=0, precision=None):
    return lax.dot_general(
        left,
        right,
        (((left_dim,), (right_dim,)), ((), ())),
        preferred_element_type=F32,
        precision=precision,
    )


def iota(shape, dim):
    return lax.broadcasted_iota(jnp.int32, shape, dim)


def dispatch_kernel(devices, assign_hbm, targ_hbm, rows_hbm, out_ref, assign_ref, targ_ref, rows_ref, sems):
    copies = [
        pltpu.make_async_copy(source, target, sems.at[i])
        for i, (source, target) in enumerate(
            ((assign_hbm, assign_ref), (targ_hbm, targ_ref), (rows_hbm, rows_ref))
        )
    ]
    for copy in copies:
        copy.start()
    copies[0].wait()
    assign = assign_ref[...]
    count, width = rows_ref.shape
    per_slot = CAP // devices
    onehot = iota((devices, count), 0) == assign
    earlier = (iota((count, count), 0) < iota((count, count), 1)).astype(BF16)
    rank = dot(onehot.astype(BF16), earlier)
    slot = jnp.sum(jnp.where(onehot, rank, 0.0), axis=0, keepdims=True)
    place = assign * per_slot + slot.astype(jnp.int32)
    here = iota((CAP, count), 0) == place
    copies[1].wait()
    targ = targ_ref[...].astype(F32).reshape(1, count)
    targ = jnp.sum(jnp.where(here, targ, 0.0), axis=1, keepdims=True)
    copies[2].wait()
    placed = dot(here.astype(BF16), rows_ref[...]).astype(BF16)
    if tight(devices):
        for i in range(width // 128):
            block = placed[:, i * 128 : (i + 1) * 128].reshape(devices, per_slot, 128)
            out_ref[:, i * per_slot : (i + 1) * per_slot, :] = block
        targ = targ.reshape(devices, per_slot, 1)
        lane = iota((devices, per_slot // 2, 128), 2)
        targ = jnp.where(lane < 64, targ[:, : per_slot // 2], targ[:, per_slot // 2 :])
        out_ref[:, width // 128 * per_slot :, :] = targ.astype(BF16)
    else:
        out_ref[:, :width] = placed
        out_ref[:, width:] = jnp.broadcast_to(targ, (CAP, 128)).astype(BF16)


def tight(devices):
    return (CAP // devices) % 16 == 0


def gram_rows_to_column(gram, row):
    parts = []
    for start in range(0, CAP, 64):
        product = gram[start : start + 64, :] * row
        folded = sum(product[:, lane : lane + 128] for lane in range(0, CAP, 128))
        parts.append(jnp.sum(folded, axis=1, keepdims=True))
    return jnp.concatenate(parts, axis=0)


def gram_column_to_row(gram, column):
    total = jnp.zeros((8, CAP), F32)
    for start in range(0, CAP, 64):
        product = gram[start : start + 64, :] * column[start : start + 64, :]
        total = total + jnp.sum(product.reshape(8, 8, CAP), axis=0)
    return jnp.sum(total, axis=0, keepdims=True)


def fit_kernel(
    blocks,
    noise_ref,
    got_ref,
    first_ref,
    second_hbm,
    pre_ref,
    grad_ref,
    xt_ref,
    ht_ref,
    loss_ref,
    hid_ref,
    feat_ref,
    gram_ref,
    x_ref,
    targ_ref,
    second_ref,
    sem,
):
    din, hid = first_ref.shape
    feat = second_hbm.shape[1]
    step = 128
    chunks = CAP // step
    second_copy = pltpu.make_async_copy(second_hbm, second_ref, sem)
    second_copy.start()
    if tight(blocks):
        per_slot = CAP // blocks
        for i in range(din // 128):
            block = got_ref[:, i * per_slot : (i + 1) * per_slot, :]
            x_ref[:, i * 128 : (i + 1) * 128] = block.reshape(CAP, 128)
        packed = got_ref[:, din // 128 * per_slot :, :].astype(F32)
        lanes = (blocks, per_slot // 2, 128)
        parts = [jnp.broadcast_to(packed[:, :, i : i + 1], lanes) for i in (0, 64)]
        targ_ref[...] = jnp.concatenate(parts, axis=1).reshape(CAP, 128)
    else:
        x_ref[...] = got_ref[:, :din]
        targ_ref[...] = got_ref[:, din:].astype(F32)

    def split_parity(source, target):
        turned = source.T.reshape(blocks // 2, 2, din // blocks, CAP)
        target[0] = turned[:, 0].reshape(din // 2, CAP)
        target[1] = turned[:, 1].reshape(din // 2, CAP)

    @pl.loop(0, chunks)
    def _(i):
        rows = pl.ds(pl.multiple_of(i * step, step), step)
        pre = dot(x_ref[rows, :], first_ref[...])
        pre_ref[rows, :] = pre
        hid_ref[rows, :] = (pre * jax.nn.sigmoid(pre)).astype(BF16)

    second_copy.wait()

    @pl.loop(0, chunks)
    def _(i):
        rows = pl.ds(pl.multiple_of(i * step, step), step)
        feat_ref[rows, :] = dot(hid_ref[rows, :], second_ref[...]).astype(BF16)

    split_parity(x_ref[...], xt_ref)
    split_parity(hid_ref[...], ht_ref)

    feats = feat_ref[...]
    gram_ref[...] = dot(feats, feats, 1, 1) * (1.0 / feat)
    gram = gram_ref[...]
    noise = noise_ref[0]
    squares = sum(
        jnp.sum((gram[i : i + 64, :] * gram[i : i + 64, :]).reshape(8, 8, CAP), axis=0)
        for i in range(0, CAP, 64)
    )
    root = jnp.sqrt(jnp.sum(squares, keepdims=True) + 1e-06)
    theta = root + noise
    inverse = 1.0 / theta
    shrink = root * inverse

    targ = targ_ref[...]
    column = targ[:, :1]
    lane = iota((CAP, 128), 1)
    sub = iota((POWERS, CAP), 0)
    columns = jnp.where(lane == 0, targ, 0.0)
    row_set = jnp.zeros((POWERS, CAP), F32)
    targ_row = targ.T[:1, :]
    row = None
    for k in range(1, POWERS - 1):
        if k % 2 == 1:
            before = targ_row if k == 1 else columns.T[k - 1 : k, :]
            row = shrink * before - gram_column_to_row(gram, column) * inverse
            row_set = row_set + jnp.where(sub == k, row, 0.0)
        else:
            before = row.T
            column = shrink * before - gram_rows_to_column(gram, row) * inverse
            columns = columns + jnp.where(lane == k, column, 0.0)
    powers = row_set + columns.T[:POWERS, :]
    moments = jnp.sum(powers * targ_row, axis=1, keepdims=True)
    last = jnp.sum(powers[7:8, :] * powers[8:9, :], axis=1, keepdims=True)
    loss_ref[...] = 0.5 * inverse * (jnp.sum(moments, axis=0, keepdims=True) + last)
    mask = (iota((POWERS, POWERS), 0) + iota((POWERS, POWERS), 1) <= POWERS - 2).astype(F32)
    sums = dot(mask, powers, precision=EXACT)
    outer = dot(powers, sums, 0, 0, precision=EXACT) + (16.0 * last / root) * gram
    high = outer.astype(BF16)
    low = (outer - high.astype(F32)).astype(BF16)
    scale = -inverse * inverse * (1.0 / feat)
    grad_ref[...] = ((dot(high, feats) + dot(low, feats)) * scale).astype(BF16)


def second_kernel(parity_ref, grad_ref, ht_ref, keep_ref, send_ref):
    parity = parity_ref[0]
    keep_ref[...] = dot(ht_ref[parity], grad_ref[...])
    send_ref[...] = dot(ht_ref[1 - parity], grad_ref[...])


def first_kernel(parity_ref, grad_ref, second_ref, pre_ref, xt_ref, keep_ref, send_ref, pgrad_ref):
    step = 128
    parity = parity_ref[0]

    @pl.loop(0, CAP // step)
    def _(i):
        rows = pl.ds(pl.multiple_of(i * step, step), step)
        hidden_grad = dot(grad_ref[rows, :], second_ref[...], 1, 1)
        pre = pre_ref[rows, :]
        sigma = jax.nn.sigmoid(pre)
        pgrad_ref[rows, :] = (hidden_grad * sigma * (1.0 + pre * (1.0 - sigma))).astype(BF16)

    send_ref[...] = dot(xt_ref[1 - parity], pgrad_ref[...])
    keep_ref[...] = dot(xt_ref[parity], pgrad_ref[...])


def split_kernel(group, leading, place_ref, *refs):
    parts, outs = refs[:-group], refs[-group:]
    place = place_ref[0]
    for d, out in enumerate(outs):
        target = jnp.bitwise_xor(place, d)
        index = (target,) if leading else (slice(None), target)
        total = parts[0][index].astype(F32)
        for part in parts[1:]:
            total = total + part[index].astype(F32)
        out[...] = total.astype(out.dtype)


def split_stage(place, parts, outer, group, own_rows, leading=False):
    columns = parts[0].shape[-1]
    shape = (*((group, outer) if leading else (outer, group)), own_rows, columns)
    made = (outer, own_rows, columns)
    return pl.pallas_call(
        functools.partial(split_kernel, group, leading),
        out_shape=[jax.ShapeDtypeStruct(made, F32 if d == 0 else BF16) for d in range(group)],
        in_specs=[SMEM] + [VMEM] * len(parts),
        out_specs=[VMEM] * group,
        cost_estimate=cost(outer * group * own_rows * columns * 1000),
        compiler_params=PARAMS,
    )(place, *[part.reshape(shape) for part in parts])


def swap(array, axis, distance):
    count = lax.axis_size(axis)
    return lax.ppermute(array, axis, [(i, i ^ distance) for i in range(count)])


def exchange(parts, axis, unit):
    return [parts[0]] + [swap(parts[d], axis, d * unit) for d in range(1, len(parts))]


def on_device(inputs, first_weight, second_weight, targets, noise_var, assignment):
    gx_count = lax.axis_size("gx")
    gy_count = lax.axis_size("gy")
    devices = gx_count * gy_count
    per_slot = CAP // devices
    rows, din = inputs.shape
    hid, feat = second_weight.shape
    own_rows = din // devices
    gx = lax.axis_index("gx")
    gy = lax.axis_index("gy")

    def scalar(x):
        return x.astype(jnp.int32).reshape(1)

    if tight(devices):
        sent_shape = packed_shape = (devices, din // 128 * per_slot + per_slot // 2, 128)
    else:
        sent_shape, packed_shape = (CAP, din + 128), (devices, per_slot, din + 128)
    sent = pl.pallas_call(
        functools.partial(dispatch_kernel, devices),
        out_shape=jax.ShapeDtypeStruct(sent_shape, BF16),
        in_specs=[ANY] * 3,
        out_specs=VMEM,
        scratch_shapes=[
            pltpu.VMEM((1, rows), jnp.int32),
            pltpu.VMEM((rows,), BF16),
            pltpu.VMEM((rows, din), BF16),
            pltpu.SemaphoreType.DMA((3,)),
        ],
        cost_estimate=cost(2 * CAP * rows * din),
        compiler_params=PARAMS,
    )(assignment.reshape(1, rows), targets, inputs)
    got = lax.all_to_all(
        sent.reshape(packed_shape), ("gx", "gy"), split_axis=0, concat_axis=0, tiled=True
    ).reshape(sent_shape)

    half = din // 2
    pre, grad, xt, ht, loss = pl.pallas_call(
        functools.partial(fit_kernel, devices),
        out_shape=[
            jax.ShapeDtypeStruct((CAP, hid), F32),
            jax.ShapeDtypeStruct((CAP, feat), BF16),
            jax.ShapeDtypeStruct((2, half, CAP), BF16),
            jax.ShapeDtypeStruct((2, half, CAP), BF16),
            jax.ShapeDtypeStruct((1, 1), F32),
        ],
        in_specs=[SMEM, VMEM, VMEM, ANY],
        out_specs=[VMEM] * 5,
        scratch_shapes=[
            pltpu.VMEM((CAP, hid), BF16),
            pltpu.VMEM((CAP, feat), BF16),
            pltpu.VMEM((CAP, CAP), F32),
            pltpu.VMEM((CAP, din), BF16),
            pltpu.VMEM((CAP, 128), F32),
            pltpu.VMEM((hid, feat), BF16),
            pltpu.SemaphoreType.DMA,
        ],
        cost_estimate=cost(8 * CAP * din * hid),
        compiler_params=PARAMS,
    )(noise_var, got, first_weight, second_weight)

    parity = scalar(gy % 2)
    keep2, send2 = pl.pallas_call(
        second_kernel,
        out_shape=[jax.ShapeDtypeStruct((half, feat), F32)] * 2,
        in_specs=[SMEM, VMEM, VMEM],
        out_specs=[VMEM] * 2,
        cost_estimate=cost(2 * CAP * hid * feat * 2),
        compiler_params=PARAMS,
    )(parity, grad, ht)
    pre, keep2, send2 = lax.optimization_barrier((pre, keep2, send2))
    keep1, send1 = pl.pallas_call(
        first_kernel,
        out_shape=[jax.ShapeDtypeStruct((half, hid), F32)] * 2,
        in_specs=[SMEM, VMEM, VMEM, VMEM, VMEM],
        out_specs=[VMEM] * 2,
        scratch_shapes=[pltpu.VMEM((CAP, hid), BF16)],
        cost_estimate=cost(2 * CAP * din * hid * 4),
        compiler_params=PARAMS,
    )(parity, grad, second_weight, pre, xt)

    plane = gy_count // 2

    def over_gy(parts, outer):
        return exchange(split_stage(scalar(gy // 2), parts, outer, plane, own_rows), "gy", 2)

    def over_gx(parts, outer):
        return exchange(split_stage(scalar(gx), parts, outer, gx_count, own_rows, True), "gx", 1)

    def added(parts):
        return sum(part.astype(F32) for part in parts).reshape(own_rows, -1)

    second_parts = [keep2, swap(send2, "gy", 1)]
    send1, second_parts[1] = lax.optimization_barrier((send1, second_parts[1]))
    first_parts = [keep1, swap(send1, "gy", 1)]
    second_parts[0], first_parts[0] = lax.optimization_barrier((second_parts[0], first_parts[0]))
    second_parts = over_gx(second_parts, plane)
    first_parts = over_gy(first_parts, gx_count)
    second_parts = over_gy(second_parts, 1)
    first_parts = over_gx(first_parts, 1)
    second_total = added(second_parts)
    first_total = added(first_parts)
    return (first_total, second_total, loss.reshape(1))


def solution(mesh):
    return jax.shard_map(
        on_device,
        mesh=mesh,
        in_specs=(
            P(("gx", "gy"), None),
            P(),
            P(),
            P(("gx", "gy")),
            P(("gx", "gy")),
            P(("gx", "gy"), None),
        ),
        out_specs=(P(("gx", "gy"), None), P(("gx", "gy"), None), P(("gx", "gy"))),
        check_vma=False,
    )
```

time: 101 us -> 92.4 us (0.915)
  waiting for transfers between devices: 49.2 us -> 41.4 us
  local copies, waits for them, and re-layouts: 4.06 us -> 6.25 us
  Pallas kernels: 19.4 us -> 17.7 us
  starting transfers between devices: 25.3 us -> 23.9 us
    ppermute x14, waiting for transfers between devices: 20.8 us -> 14.4 us  [swap(): return lax.ppermute(array, axis, [(i, i ^ distance) for i in range(count)])]
    unnamed x8 -> x16, local copies, waits for them, and re-layouts: 3.31 us -> 6.25 us
    pallas_call x3 -> x7, Pallas kernels: 17.7 us -> 15.8 us  [the longest x1 8.8 us: on_device(): pl.pallas_call(functools.partial(fit_kernel, devices), out_shape=[jax.Sha...]
    all_to_all x1, waiting for transfers between devices: 28.4 us -> 27 us  [on_device(): lax.all_to_all(sent.reshape(packed_shape), ('gx', 'gy'), split_axis=0, co...]
    ppermute x14, starting transfers between devices: 18 us -> 16.6 us  [swap(): return lax.ppermute(array, axis, [(i, i ^ distance) for i in range(count)])]
  transfers between devices with their start and end apart: 15 -> 15, of which waited for: 7 -> 4; matrix products, arithmetic and copies ran while one was open for 1% -> 1% of each run, Pallas kernels for 0% -> 7%
where the time goes in v1:
time: 92.4 us; the launch traced here: 92 us
  waiting for transfers between devices  41.4 us (45%)
  starting transfers between devices  23.9 us (26%)
  Pallas kernels  17.7 us (19%)
  local copies, waits for them, and re-layouts  6.25 us (7%)
  between operations  1.38 us (1%)
  other arithmetic  1.34 us (1%)
    all_to_all x1, waiting for transfers between devices, on_device(): lax.all_to_all(sent.reshape(packed_shape), ('gx', 'gy'), split_axis=0, co...  27 us
    ppermute x14, starting transfers between devices, swap(): return lax.ppermute(array, axis, [(i, i ^ distance) for i in range(count)])  16.6 us
    ppermute x14, waiting for transfers between devices, swap(): return lax.ppermute(array, axis, [(i, i ^ distance) for i in range(count)])  14.4 us
    pallas_call x1, Pallas kernels, on_device(): pl.pallas_call(functools.partial(fit_kernel, devices), out_shape=[jax.Sha...  8.8 us
    all_to_all x1, starting transfers between devices, on_device(): lax.all_to_all(sent.reshape(packed_shape), ('gx', 'gy'), split_axis=0, co...  7.3 us
    unnamed x16, local copies, waits for them, and re-layouts  6.25 us
    pallas_call x1, Pallas kernels, on_device(): pl.pallas_call(first_kernel, out_shape=[jax.ShapeDtypeStruct((half, hid),...  4.11 us
    pallas_call x4, Pallas kernels, split_stage(): pl.pallas_call(functools.partial(split_kernel, group, leading), out_shape...  2.13 us
  transfers between devices with their start and end apart: 15, of which 4 were waited for; matrix products, arithmetic and copies ran while one was open for 1% of the time, Pallas kernels for 7%

profile of v1, /device:TPU:0, one launch (start us, length us, event | category | flops | bytes accessed | tf_op | source)
XLA Modules:
  0.0 92.0 jit_solution(6379346222142984432)
XLA Ops:
  0.6 1.0 %copy-done.2 = bf16[256,1024]{1,0:T(8,128)(2,1)S(1)} copy-done((bf16[256,1024]{1,0:T(8,128)(2,1)S(1)}, bf16[256,1024]{1,0:T(8,128)(2,1)}, u32[]{:S(2)}) %copy-start.2) | copy-done | bytes 524312
  1.7 0.7 copy-done.3
  2.4 0.7 copy-done.4
  3.0 1.9 %shard_map.85 = bf16[32,136,128]{2,1,0:T(8,128)(2,1)} custom-call(s32[1,256]{1,0:T(1,128)S(1)} %bitcast.32, bf16[256]{0:T(256)(128)(2,1)S(1)} %copy-done.4, bf16[256,1024]{1,0:T(8,128)(2,1)S(1)} %copy-done.2), custom_call_target="tpu_custom_call" | custom-call | flops 268435456 | tf_op jit(solution)/shard_map/pallas_call | solution.py:275
  5.0 7.3 %all-to-all-start = ((bf16[32,136,128]{2,1,0:T(8,128)(2,1)}), bf16[32,136,128]{2,1,0:T(8,128)(2,1)S(1)}, u32[]{:S(2)}, u32[]{:S(2)}) async-start(bf16[32,136,128]{2,1,0:T(8,128)(2,1)} %shard_map.85), calls=%async_computation | async-start | bytes 2228224 | tf_op jit(solution)/shard_map/all_to_all | solution.py:289
  12.9 27.0 %all-to-all-done.got_ref = bf16[32,136,128]{2,1,0:T(8,128)(2,1)S(1)} async-done(((bf16[32,136,128]{2,1,0:T(8,128)(2,1)}), bf16[32,136,128]{2,1,0:T(8,128)(2,1)S(1)}, u32[]{:S(2)}, u32[]{:S(2)}) %all-to-all-start) | async-done | bytes 1114144 | tf_op jit(solution)/shard_map/all_to_all | solution.py:289
  39.9 1.2 %copy-done.6 = bf16[1024,512]{1,0:T(8,128)(2,1)S(1)} copy-done((bf16[1024,512]{1,0:T(8,128)(2,1)S(1)}, bf16[1024,512]{1,0:T(8,128)(2,1)}, u32[]{:S(2)}) %copy-start.6) | copy-done | bytes 1048600
  41.1 8.8 %shard_map.86 = (f32[512,1024]{1,0:T(8,128)S(1)}, bf16[512,512]{1,0:T(8,128)(2,1)S(1)}, bf16[2,512,512]{2,1,0:T(8,128)(2,1)S(1)}, bf16[2,512,512]{2,1,0:T(8,128)(2,1)S(1)}, f32[1,1]{1,0:T(1,128)}) custom-call(f32[1]{0:T(128)S(6)} %copy.9.noise_ref, bf16[32,136,128]{2,1,0:T(8,128)(2,1)S(1)} %all-to-all-done.got_ref, bf16[1024,1024]{1,0:T(8,128)(2,1)S(1)} %copy-done.5, ...), custom_call_target="tpu_custom_call" | custom-call | flops 4294967296 | tf_op jit(solution)/shard_map/pallas_call | solution.py:294
  49.9 0.0 copy-start.7
  50.0 0.7 shard_map.87
  50.7 0.1 collective-permute-start
  50.7 0.4 copy-done.7
  51.2 4.1 %shard_map.88 = (f32[512,1024]{1,0:T(8,128)S(1)}, f32[512,1024]{1,0:T(8,128)}) custom-call(s32[1]{0:T(128)} %bitcast.3.parity_ref, bf16[512,512]{1,0:T(8,128)(2,1)S(1)} %get-tuple-element.36.grad_ref, bf16[1024,512]{1,0:T(8,128)(2,1)S(1)} %copy-done.7, f32[512,1024]{1,0:T(8,128)S(1)} %get-tuple-element.41.pre_ref, ...), custom_call_target="tpu_custom_call" | custom-call | flops 4294967296 | tf_op jit(solution)/shard_map/pallas_call | solution.py:328
  55.3 0.0 collective-permute-done
  55.3 1.0 %copy-done = f32[512,512]{1,0:T(8,128)} copy-done((f32[512,512]{1,0:T(8,128)}, f32[512,512]{1,0:T(8,128)S(1)}, u32[]{:S(2)}) %copy-start) | copy-done | bytes 1048600
  56.3 0.1 collective-permute-start.1
  56.4 1.2 %copy-done.1 = f32[512,512]{1,0:T(8,128)S(1)} copy-done((f32[512,512]{1,0:T(8,128)S(1)}, f32[512,512]{1,0:T(8,128)}, u32[]{:S(2)}) %copy-start.1) | copy-done | bytes 1048600
  57.6 0.2 shard_map.91
  57.8 0.9 %collective-permute-start.8 = (bf16[4,32,512]{2,1,0:T(8,128)(2,1)S(1)}, bf16[4,32,512]{2,1,0:T(8,128)(2,1)S(1)}, u32[]{:S(2)}, u32[]{:S(2)}) collective-permute-start(bf16[4,32,512]{2,1,0:T(8,128)(2,1)S(1)} %get-tuple-element.59), channel_id=1, source_target_pairs={{0,8},{8,0},{16,24},{24,16},{1,9},{9,1},{17,25},{25,17},{2,10},{10... | collective-permute-start | bytes 393224 | tf_op jit(solution)/shard_map/ppermute | solution.py:250
  58.7 2.1 %collective-permute-done.1 = f32[512,1024]{1,0:T(8,128)} collective-permute-done((f32[512,1024]{1,0:T(8,128)}, f32[512,1024]{1,0:T(8,128)}, u32[]{:S(2)}, u32[]{:S(2)}) %collective-permute-start.1) | collective-permute-done | bytes 2097184 | tf_op jit(solution)/shard_map/ppermute | solution.py:250
  60.8 1.8 %shard_map.89 = (f32[4,32,1024]{2,1,0:T(8,128)S(1)}, bf16[4,32,1024]{2,1,0:T(8,128)(2,1)S(1)}, bf16[4,32,1024]{2,1,0:T(8,128)(2,1)S(1)}, bf16[4,32,1024]{2,1,0:T(8,128)(2,1)S(1)}) custom-call(s32[1]{0:T(128)} %bitcast.1.place_ref, f32[4,4,32,1024]{3,2,1,0:T(8,128)S(1)} %bitcast.21, f32[4,4,32,1024]{3,2,1,0:T(8,128)} %bitcast.5.refs_1_), custom_call_target="tpu_custom_call" | custom-call | flops 524288000 | tf_op jit(solution)/shard_map/pallas_call | solution.py:238
  62.6 1.5 %collective-permute-start.2 = (bf16[4,32,1024]{2,1,0:T(8,128)(2,1)S(1)}, bf16[4,32,1024]{2,1,0:T(8,128)(2,1)S(1)}, u32[]{:S(2)}, u32[]{:S(2)}) collective-permute-start(bf16[4,32,1024]{2,1,0:T(8,128)(2,1)S(1)} %get-tuple-element.49), channel_id=1, source_target_pairs={{0,2},{1,3},{2,0},{3,1},{4,6},{5,7},{6,4},{7,5},{8,10},{9,11},{10,... | collective-permute-start | bytes 786440 | tf_op jit(solution)/shard_map/ppermute | solution.py:250
  64.1 1.5 %collective-permute-start.3 = (bf16[4,32,1024]{2,1,0:T(8,128)(2,1)S(1)}, bf16[4,32,1024]{2,1,0:T(8,128)(2,1)S(1)}, u32[]{:S(2)}, u32[]{:S(2)}) collective-permute-start(bf16[4,32,1024]{2,1,0:T(8,128)(2,1)S(1)} %get-tuple-element.50), channel_id=1, source_target_pairs={{0,4},{1,5},{2,6},{3,7},{4,0},{5,1},{6,2},{7,3},{8,12},{9,13},{10,... | collective-permute-start | bytes 786440 | tf_op jit(solution)/shard_map/ppermute | solution.py:250
  65.6 0.5 collective-permute-start.4
  66.1 1.2 %collective-permute-start.9 = (bf16[4,32,512]{2,1,0:T(8,128)(2,1)S(1)}, bf16[4,32,512]{2,1,0:T(8,128)(2,1)S(1)}, u32[]{:S(2)}, u32[]{:S(2)}) collective-permute-start(bf16[4,32,512]{2,1,0:T(8,128)(2,1)S(1)} %get-tuple-element.60), channel_id=1, source_target_pairs={{0,16},{8,24},{16,0},{24,8},{1,17},{9,25},{17,1},{25,9},{2,18},{10... | collective-permute-start | bytes 393224 | tf_op jit(solution)/shard_map/ppermute | solution.py:250
  67.3 0.0 collective-permute-done.8
  67.3 1.8 %collective-permute-start.10 = (bf16[4,32,512]{2,1,0:T(8,128)(2,1)S(1)}, bf16[4,32,512]{2,1,0:T(8,128)(2,1)S(1)}, u32[]{:S(2)}, u32[]{:S(2)}) collective-permute-start(bf16[4,32,512]{2,1,0:T(8,128)(2,1)S(1)} %get-tuple-element.61), channel_id=1, source_target_pairs={{0,24},{8,16},{16,8},{24,0},{1,25},{9,17},{17,9},{25,1},{2,26},{10... | collective-permute-start | bytes 393224 | tf_op jit(solution)/shard_map/ppermute | solution.py:250
  69.1 8.6 %collective-permute-done.9 = bf16[4,32,512]{2,1,0:T(8,128)(2,1)S(1)} collective-permute-done((bf16[4,32,512]{2,1,0:T(8,128)(2,1)S(1)}, bf16[4,32,512]{2,1,0:T(8,128)(2,1)S(1)}, u32[]{:S(2)}, u32[]{:S(2)}) %collective-permute-start.9) | collective-permute-done | bytes 131104 | tf_op jit(solution)/shard_map/ppermute | solution.py:250
  77.8 0.0 collective-permute-done.10
  77.8 0.1 shard_map.92
  77.8 1.5 %collective-permute-start.11 = (bf16[1,32,512]{2,1,0:T(8,128)(2,1)S(1)}, bf16[1,32,512]{2,1,0:T(8,128)(2,1)S(1)}, u32[]{:S(2)}, u32[]{:S(2)}) collective-permute-start(bf16[1,32,512]{2,1,0:T(8,128)(2,1)S(1)} %get-tuple-element.63), channel_id=1, source_target_pairs={{0,2},{1,3},{2,0},{3,1},{4,6},{5,7},{6,4},{7,5},{8,10},{9,11},{10,... | collective-permute-start | bytes 98312 | tf_op jit(solution)/shard_map/ppermute | solution.py:250
  79.3 0.4 collective-permute-start.12
  79.7 0.0 collective-permute-done.2
  79.7 1.7 %collective-permute-start.13 = (bf16[1,32,512]{2,1,0:T(8,128)(2,1)S(1)}, bf16[1,32,512]{2,1,0:T(8,128)(2,1)S(1)}, u32[]{:S(2)}, u32[]{:S(2)}) collective-permute-start(bf16[1,32,512]{2,1,0:T(8,128)(2,1)S(1)} %get-tuple-element.65), channel_id=1, source_target_pairs={{0,6},{1,7},{2,4},{3,5},{4,2},{5,3},{6,0},{7,1},{8,14},{9,15},{10,... | collective-permute-start | bytes 98312 | tf_op jit(solution)/shard_map/ppermute | solution.py:250
  81.4 0.0 collective-permute-done.3
  81.4 0.0 collective-permute-done.4
  81.4 0.1 shard_map.90
  81.5 3.0 %collective-permute-start.5 = (bf16[1,32,1024]{2,1,0:T(8,128)(2,1)S(1)}, bf16[1,32,1024]{2,1,0:T(8,128)(2,1)S(1)}, u32[]{:S(2)}, u32[]{:S(2)}) collective-permute-start(bf16[1,32,1024]{2,1,0:T(8,128)(2,1)S(1)} %get-tuple-element.53), channel_id=1, source_target_pairs={{0,8},{8,0},{16,24},{24,16},{1,9},{9,1},{17,25},{25,17},{2,10},{10... | collective-permute-start | bytes 196616 | tf_op jit(solution)/shard_map/ppermute | solution.py:250
  84.5 0.0 collective-permute-start.6
  84.5 0.0 collective-permute-done.11
  84.5 2.4 %collective-permute-start.7 = (bf16[1,32,1024]{2,1,0:T(8,128)(2,1)S(1)}, bf16[1,32,1024]{2,1,0:T(8,128)(2,1)S(1)}, u32[]{:S(2)}, u32[]{:S(2)}) collective-permute-start(bf16[1,32,1024]{2,1,0:T(8,128)(2,1)S(1)} %get-tuple-element.55), channel_id=1, source_target_pairs={{0,24},{8,16},{16,8},{24,0},{1,25},{9,17},{17,9},{25,1},{2,26},{10... | collective-permute-start | bytes 196616 | tf_op jit(solution)/shard_map/ppermute | solution.py:250
  87.0 0.0 collective-permute-done.12
  87.0 0.0 collective-permute-done.13
  87.0 0.6 add_bitcast_fusion.1
  87.6 0.0 collective-permute-done.5
  87.6 3.7 %collective-permute-done.6 = bf16[1,32,1024]{2,1,0:T(8,128)(2,1)S(1)} collective-permute-done((bf16[1,32,1024]{2,1,0:T(8,128)(2,1)S(1)}, bf16[1,32,1024]{2,1,0:T(8,128)(2,1)S(1)}, u32[]{:S(2)}, u32[]{:S(2)}) %collective-permute-start.6) | collective-permute-done | bytes 65568 | tf_op jit(solution)/shard_map/ppermute | solution.py:250
  91.3 0.0 collective-permute-done.7
  91.3 0.7 add_bitcast_fusion
  (8 shorter events, 0.0 us)
Async XLA Ops:
  0.6 1.0 %copy-start.2 = (bf16[256,1024]{1,0:T(8,128)(2,1)S(1)}, bf16[256,1024]{1,0:T(8,128)(2,1)}, u32[]{:S(2)}) copy-start(bf16[256,1024]{1,0:T(8,128)(2,1)} %rows_hbm.1) | copy-start | bytes 1572868
  1.7 0.7 copy-start.3
  2.4 0.7 copy-start.4
  3.0 36.9 %copy-start.5 = (bf16[1024,1024]{1,0:T(8,128)(2,1)S(1)}, bf16[1024,1024]{1,0:T(8,128)(2,1)}, u32[]{:S(2)}) copy-start(bf16[1024,1024]{1,0:T(8,128)(2,1)} %first_ref.1) | copy-start | bytes 6291460
  5.0 35.0 %all-to-all-start = ((bf16[32,136,128]{2,1,0:T(8,128)(2,1)}), bf16[32,136,128]{2,1,0:T(8,128)(2,1)S(1)}, u32[]{:S(2)}, u32[]{:S(2)}) async-start(bf16[32,136,128]{2,1,0:T(8,128)(2,1)} %shard_map.85), calls=%async_computation | async-start | bytes 2228224 | tf_op jit(solution)/shard_map/all_to_all | solution.py:289
  39.9 1.2 %copy-start.6 = (bf16[1024,512]{1,0:T(8,128)(2,1)S(1)}, bf16[1024,512]{1,0:T(8,128)(2,1)}, u32[]{:S(2)}) copy-start(bf16[1024,512]{1,0:T(8,128)(2,1)} %second_ref.1) | copy-start | bytes 3145732
  49.9 1.2 %copy-start.7 = (bf16[1024,512]{1,0:T(8,128)(2,1)S(1)}, bf16[1024,512]{1,0:T(8,128)(2,1)}, u32[]{:S(2)}) copy-start(bf16[1024,512]{1,0:T(8,128)(2,1)} %second_ref.1) | copy-start | bytes 3145732
  50.7 4.6 %collective-permute-start = (f32[512,512]{1,0:T(8,128)S(1)}, f32[512,512]{1,0:T(8,128)S(1)}, u32[]{:S(2)}, u32[]{:S(2)}) collective-permute-start(f32[512,512]{1,0:T(8,128)S(1)} %get-tuple-element.46), channel_id=1, source_target_pairs={{0,1},{1,0},{2,3},{3,2},{4,5},{5,4},{6,7},{7,6},{8,9},{9,8},{10,11... | collective-permute-start | bytes 3145736 | tf_op jit(solution)/shard_map/ppermute | solution.py:250
  55.3 1.0 %copy-start = (f32[512,512]{1,0:T(8,128)}, f32[512,512]{1,0:T(8,128)S(1)}, u32[]{:S(2)}) copy-start(f32[512,512]{1,0:T(8,128)S(1)} %collective-permute-done) | copy-start | bytes 3145732
  56.3 4.5 %collective-permute-start.1 = (f32[512,1024]{1,0:T(8,128)}, f32[512,1024]{1,0:T(8,128)}, u32[]{:S(2)}, u32[]{:S(2)}) collective-permute-start(f32[512,1024]{1,0:T(8,128)} %get-tuple-element.47), channel_id=1, source_target_pairs={{0,1},{1,0},{2,3},{3,2},{4,5},{5,4},{6,7},{7,6},{8,9},{9,8},{10,11... | collective-permute-start | bytes 6291464 | tf_op jit(solution)/shard_map/ppermute | solution.py:250
  56.4 1.2 %copy-start.1 = (f32[512,512]{1,0:T(8,128)S(1)}, f32[512,512]{1,0:T(8,128)}, u32[]{:S(2)}) copy-start(f32[512,512]{1,0:T(8,128)} %copy-done) | copy-start | bytes 3145732
  57.8 9.5 %collective-permute-start.8 = (bf16[4,32,512]{2,1,0:T(8,128)(2,1)S(1)}, bf16[4,32,512]{2,1,0:T(8,128)(2,1)S(1)}, u32[]{:S(2)}, u32[]{:S(2)}) collective-permute-start(bf16[4,32,512]{2,1,0:T(8,128)(2,1)S(1)} %get-tuple-element.59), channel_id=1, source_target_pairs={{0,8},{8,0},{16,24},{24,16},{1,9},{9,1},{17,25},{25,17},{2,10},{10... | collective-permute-start | bytes 393224 | tf_op jit(solution)/shard_map/ppermute | solution.py:250
  62.6 17.1 %collective-permute-start.2 = (bf16[4,32,1024]{2,1,0:T(8,128)(2,1)S(1)}, bf16[4,32,1024]{2,1,0:T(8,128)(2,1)S(1)}, u32[]{:S(2)}, u32[]{:S(2)}) collective-permute-start(bf16[4,32,1024]{2,1,0:T(8,128)(2,1)S(1)} %get-tuple-element.49), channel_id=1, source_target_pairs={{0,2},{1,3},{2,0},{3,1},{4,6},{5,7},{6,4},{7,5},{8,10},{9,11},{10,... | collective-permute-start | bytes 786440 | tf_op jit(solution)/shard_map/ppermute | solution.py:250
  64.1 17.3 %collective-permute-start.3 = (bf16[4,32,1024]{2,1,0:T(8,128)(2,1)S(1)}, bf16[4,32,1024]{2,1,0:T(8,128)(2,1)S(1)}, u32[]{:S(2)}, u32[]{:S(2)}) collective-permute-start(bf16[4,32,1024]{2,1,0:T(8,128)(2,1)S(1)} %get-tuple-element.50), channel_id=1, source_target_pairs={{0,4},{1,5},{2,6},{3,7},{4,0},{5,1},{6,2},{7,3},{8,12},{9,13},{10,... | collective-permute-start | bytes 786440 | tf_op jit(solution)/shard_map/ppermute | solution.py:250
  65.6 15.8 %collective-permute-start.4 = (bf16[4,32,1024]{2,1,0:T(8,128)(2,1)S(1)}, bf16[4,32,1024]{2,1,0:T(8,128)(2,1)S(1)}, u32[]{:S(2)}, u32[]{:S(2)}) collective-permute-start(bf16[4,32,1024]{2,1,0:T(8,128)(2,1)S(1)} %get-tuple-element.51), channel_id=1, source_target_pairs={{0,6},{1,7},{2,4},{3,5},{4,2},{5,3},{6,0},{7,1},{8,14},{9,15},{10,... | collective-permute-start | bytes 786440 | tf_op jit(solution)/shard_map/ppermute | solution.py:250
  66.1 11.6 %collective-permute-start.9 = (bf16[4,32,512]{2,1,0:T(8,128)(2,1)S(1)}, bf16[4,32,512]{2,1,0:T(8,128)(2,1)S(1)}, u32[]{:S(2)}, u32[]{:S(2)}) collective-permute-start(bf16[4,32,512]{2,1,0:T(8,128)(2,1)S(1)} %get-tuple-element.60), channel_id=1, source_target_pairs={{0,16},{8,24},{16,0},{24,8},{1,17},{9,25},{17,1},{25,9},{2,18},{10... | collective-permute-start | bytes 393224 | tf_op jit(solution)/shard_map/ppermute | solution.py:250
  67.3 10.5 %collective-permute-start.10 = (bf16[4,32,512]{2,1,0:T(8,128)(2,1)S(1)}, bf16[4,32,512]{2,1,0:T(8,128)(2,1)S(1)}, u32[]{:S(2)}, u32[]{:S(2)}) collective-permute-start(bf16[4,32,512]{2,1,0:T(8,128)(2,1)S(1)} %get-tuple-element.61), channel_id=1, source_target_pairs={{0,24},{8,16},{16,8},{24,0},{1,25},{9,17},{17,9},{25,1},{2,26},{10... | collective-permute-start | bytes 393224 | tf_op jit(solution)/shard_map/ppermute | solution.py:250
  77.8 6.7 %collective-permute-start.11 = (bf16[1,32,512]{2,1,0:T(8,128)(2,1)S(1)}, bf16[1,32,512]{2,1,0:T(8,128)(2,1)S(1)}, u32[]{:S(2)}, u32[]{:S(2)}) collective-permute-start(bf16[1,32,512]{2,1,0:T(8,128)(2,1)S(1)} %get-tuple-element.63), channel_id=1, source_target_pairs={{0,2},{1,3},{2,0},{3,1},{4,6},{5,7},{6,4},{7,5},{8,10},{9,11},{10,... | collective-permute-start | bytes 98312 | tf_op jit(solution)/shard_map/ppermute | solution.py:250
  79.3 7.7 %collective-permute-start.12 = (bf16[1,32,512]{2,1,0:T(8,128)(2,1)S(1)}, bf16[1,32,512]{2,1,0:T(8,128)(2,1)S(1)}, u32[]{:S(2)}, u32[]{:S(2)}) collective-permute-start(bf16[1,32,512]{2,1,0:T(8,128)(2,1)S(1)} %get-tuple-element.64), channel_id=1, source_target_pairs={{0,4},{1,5},{2,6},{3,7},{4,0},{5,1},{6,2},{7,3},{8,12},{9,13},{10,... | collective-permute-start | bytes 98312 | tf_op jit(solution)/shard_map/ppermute | solution.py:250
  79.7 7.3 %collective-permute-start.13 = (bf16[1,32,512]{2,1,0:T(8,128)(2,1)S(1)}, bf16[1,32,512]{2,1,0:T(8,128)(2,1)S(1)}, u32[]{:S(2)}, u32[]{:S(2)}) collective-permute-start(bf16[1,32,512]{2,1,0:T(8,128)(2,1)S(1)} %get-tuple-element.65), channel_id=1, source_target_pairs={{0,6},{1,7},{2,4},{3,5},{4,2},{5,3},{6,0},{7,1},{8,14},{9,15},{10,... | collective-permute-start | bytes 98312 | tf_op jit(solution)/shard_map/ppermute | solution.py:250
  81.5 6.1 %collective-permute-start.5 = (bf16[1,32,1024]{2,1,0:T(8,128)(2,1)S(1)}, bf16[1,32,1024]{2,1,0:T(8,128)(2,1)S(1)}, u32[]{:S(2)}, u32[]{:S(2)}) collective-permute-start(bf16[1,32,1024]{2,1,0:T(8,128)(2,1)S(1)} %get-tuple-element.53), channel_id=1, source_target_pairs={{0,8},{8,0},{16,24},{24,16},{1,9},{9,1},{17,25},{25,17},{2,10},{10... | collective-permute-start | bytes 196616 | tf_op jit(solution)/shard_map/ppermute | solution.py:250
  84.5 6.8 %collective-permute-start.6 = (bf16[1,32,1024]{2,1,0:T(8,128)(2,1)S(1)}, bf16[1,32,1024]{2,1,0:T(8,128)(2,1)S(1)}, u32[]{:S(2)}, u32[]{:S(2)}) collective-permute-start(bf16[1,32,1024]{2,1,0:T(8,128)(2,1)S(1)} %get-tuple-element.54), channel_id=1, source_target_pairs={{0,16},{8,24},{16,0},{24,8},{1,17},{9,25},{17,1},{25,9},{2,18},{10... | collective-permute-start | bytes 196616 | tf_op jit(solution)/shard_map/ppermute | solution.py:250
  84.5 6.8 %collective-permute-start.7 = (bf16[1,32,1024]{2,1,0:T(8,128)(2,1)S(1)}, bf16[1,32,1024]{2,1,0:T(8,128)(2,1)S(1)}, u32[]{:S(2)}, u32[]{:S(2)}) collective-permute-start(bf16[1,32,1024]{2,1,0:T(8,128)(2,1)S(1)} %get-tuple-element.55), channel_id=1, source_target_pairs={{0,24},{8,16},{16,8},{24,0},{1,25},{9,17},{17,9},{25,1},{2,26},{10... | collective-permute-start | bytes 196616 | tf_op jit(solution)/shard_map/ppermute | solution.py:250

commit v2 on v1

v2 whole, which is shorter than its diff:
```python
import functools

import jax
import jax.numpy as jnp
from jax import lax
from jax.experimental import pallas as pl
from jax.experimental.pallas import tpu as pltpu
from jax.sharding import PartitionSpec as P

CAP = 512
POWERS = 16
BF16 = jnp.bfloat16
F32 = jnp.float32
EXACT = lax.Precision.HIGHEST
VMEM = pl.BlockSpec(memory_space=pltpu.VMEM)
SMEM = pl.BlockSpec(memory_space=pltpu.SMEM)
HBM = pl.BlockSpec(memory_space=pltpu.HBM)
PARAMS = pltpu.CompilerParams(vmem_limit_bytes=24 * 1024 * 1024)


def cost(work):
    return pl.CostEstimate(flops=int(work), bytes_accessed=0, transcendentals=0)


def dot(left, right, left_dim=1, right_dim=0, precision=None):
    return lax.dot_general(
        left,
        right,
        (((left_dim,), (right_dim,)), ((), ())),
        preferred_element_type=F32,
        precision=precision,
    )


def iota(shape, dim):
    return lax.broadcasted_iota(jnp.int32, shape, dim)


def dispatch_kernel(devices, assign_hbm, targ_hbm, rows_hbm, out_ref, assign_ref, targ_ref, rows_ref, sems):
    copies = [
        pltpu.make_async_copy(source, target, sems.at[i])
        for i, (source, target) in enumerate(
            ((assign_hbm, assign_ref), (targ_hbm, targ_ref), (rows_hbm, rows_ref))
        )
    ]
    for copy in copies:
        copy.start()
    copies[0].wait()
    assign = assign_ref[...]
    count, width = rows_ref.shape
    per_slot = CAP // devices
    onehot = iota((devices, count), 0) == assign
    earlier = (iota((count, count), 0) < iota((count, count), 1)).astype(BF16)
    rank = dot(onehot.astype(BF16), earlier)
    slot = jnp.sum(jnp.where(onehot, rank, 0.0), axis=0, keepdims=True)
    place = assign * per_slot + slot.astype(jnp.int32)
    here = iota((CAP, count), 0) == place
    copies[1].wait()
    targ = targ_ref[...].astype(F32).reshape(1, count)
    targ = jnp.sum(jnp.where(here, targ, 0.0), axis=1, keepdims=True)
    copies[2].wait()
    placed = dot(here.astype(BF16), rows_ref[...]).astype(BF16)
    if tight(devices):
        for i in range(width // 128):
            block = placed[:, i * 128 : (i + 1) * 128].reshape(devices, per_slot, 128)
            out_ref[:, i * per_slot : (i + 1) * per_slot, :] = block
        targ = targ.reshape(devices, per_slot, 1)
        lane = iota((devices, per_slot // 2, 128), 2)
        targ = jnp.where(lane < 64, targ[:, : per_slot // 2], targ[:, per_slot // 2 :])
        out_ref[:, width // 128 * per_slot :, :] = targ.astype(BF16)
    else:
        out_ref[:, :width] = placed
        out_ref[:, width:] = jnp.broadcast_to(targ, (CAP, 128)).astype(BF16)


def tight(devices):
    return (CAP // devices) % 16 == 0


def unpack_kernel(devices, got_ref, x_ref, targ_ref, xt_ref):
    din = x_ref.shape[1]
    if tight(devices):
        per_slot = CAP // devices
        for i in range(din // 128):
            block = got_ref[:, i * per_slot : (i + 1) * per_slot, :]
            x_ref[:, i * 128 : (i + 1) * 128] = block.reshape(CAP, 128)
        packed = got_ref[:, din // 128 * per_slot :, :].astype(F32)
        lanes = (devices, per_slot // 2, 128)
        parts = [jnp.broadcast_to(packed[:, :, i : i + 1], lanes) for i in (0, 64)]
        targ_ref[...] = jnp.concatenate(parts, axis=1).reshape(CAP, 128)
    else:
        x_ref[...] = got_ref[:, :din]
        targ_ref[...] = got_ref[:, din:].astype(F32)
    split_parity(devices, x_ref[...], xt_ref)


def split_parity(blocks, source, target):
    width = source.shape[1]
    turned = source.T.reshape(blocks // 2, 2, width // blocks, CAP)
    target[0] = turned[:, 0].reshape(width // 2, CAP)
    target[1] = turned[:, 1].reshape(width // 2, CAP)


def row_to_column(gram, row):
    parts = []
    for start in range(0, CAP, 64):
        product = gram[start : start + 64, :] * row
        folded = sum(product[:, lane : lane + 128] for lane in range(0, CAP, 128))
        parts.append(jnp.sum(folded, axis=1, keepdims=True))
    return jnp.concatenate(parts, axis=0)


def column_to_row(gram, column):
    total = jnp.zeros((8, CAP), F32)
    for start in range(0, CAP, 64):
        product = gram[start : start + 64, :] * column[start : start + 64, :]
        total = total + jnp.sum(product.reshape(8, 8, CAP), axis=0)
    return jnp.sum(total, axis=0, keepdims=True)


def fit_kernel(
    blocks,
    noise_ref,
    x_ref,
    targ_ref,
    first_ref,
    second_ref,
    pre_ref,
    grad_ref,
    ht_ref,
    loss_ref,
    hid_ref,
    feat_ref,
    gram_ref,
    resid_ref,
):
    hid = first_ref.shape[1]
    feat = second_ref.shape[1]
    step = 256
    for i in range(0, hid, step):
        pre = dot(x_ref[...], first_ref[:, i : i + step])
        pre_ref[:, i : i + step] = pre
        hid_ref[:, i : i + step] = (pre * jax.nn.sigmoid(pre)).astype(BF16)
    for i in range(0, feat, step):
        feat_ref[:, i : i + step] = dot(hid_ref[...], second_ref[:, i : i + step]).astype(BF16)
    split_parity(blocks, hid_ref[...], ht_ref)

    feats = feat_ref[...]
    gram_ref[...] = dot(feats, feats, 1, 1) * (1.0 / feat)
    gram = gram_ref[...]
    noise = noise_ref[0]
    squares = sum(
        jnp.sum((gram[i : i + 64, :] * gram[i : i + 64, :]).reshape(8, 8, CAP), axis=0)
        for i in range(0, CAP, 64)
    )
    root = jnp.sqrt(jnp.sum(squares, keepdims=True) + 1e-06)
    theta = root + noise
    inverse = 1.0 / theta
    diagonal = iota((CAP, CAP), 0) == iota((CAP, CAP), 1)
    resid_ref[...] = (jnp.where(diagonal, root, 0.0) - gram) * inverse
    resid = resid_ref

    targ = targ_ref[...]
    column = targ[:, :1]
    lane = iota((CAP, 128), 1)
    sub = iota((POWERS, CAP), 0)
    columns = jnp.where(lane == 0, targ, 0.0)
    row_set = jnp.zeros((POWERS, CAP), F32)
    targ_row = targ.T[:1, :]
    for k in range(1, POWERS - 1):
        if k % 2 == 1:
            row = column_to_row(resid, column)
            row_set = row_set + jnp.where(sub == k, row, 0.0)
        else:
            column = row_to_column(resid, row)
            columns = columns + jnp.where(lane == k, column, 0.0)
    powers = row_set + columns.T[:POWERS, :]
    moments = jnp.sum(powers * targ_row, axis=1, keepdims=True)
    last = jnp.sum(powers[7:8, :] * powers[8:9, :], axis=1, keepdims=True)
    loss_ref[...] = 0.5 * inverse * (jnp.sum(moments, axis=0, keepdims=True) + last)
    mask = (iota((POWERS, POWERS), 0) + iota((POWERS, POWERS), 1) <= POWERS - 2).astype(F32)
    sums = dot(mask, powers, precision=EXACT)
    outer = dot(powers, sums, 0, 0, precision=EXACT) + (16.0 * last / root) * gram
    high = outer.astype(BF16)
    low = (outer - high.astype(F32)).astype(BF16)
    scale = -inverse * inverse * (1.0 / feat)
    grad_ref[...] = ((dot(high, feats) + dot(low, feats)) * scale).astype(BF16)


def second_kernel(grad_ref, ht_ref, keep_ref, send_ref):
    parity = lax.axis_index("gy") % 2
    keep_ref[...] = dot(ht_ref[parity], grad_ref[...])
    send_ref[...] = dot(ht_ref[1 - parity], grad_ref[...]).astype(BF16)


def first_kernel(grad_ref, second_ref, pre_ref, xt_ref, keep_ref, send_ref):
    step = 256
    parity = lax.axis_index("gy") % 2
    for i in range(0, pre_ref.shape[1], step):
        hidden_grad = dot(grad_ref[...], second_ref[i : i + step, :], 1, 1)
        pre = pre_ref[:, i : i + step]
        sigma = jax.nn.sigmoid(pre)
        pre_grad = (hidden_grad * sigma * (1.0 + pre * (1.0 - sigma))).astype(BF16)
        send_ref[:, i : i + step] = dot(xt_ref[1 - parity], pre_grad).astype(BF16)
        keep_ref[:, i : i + step] = dot(xt_ref[parity], pre_grad)


def split_kernel(group, leading, axis, unit, *refs):
    parts, outs = refs[:-group], refs[-group:]
    place = lax.axis_index(axis) // unit
    for d, out in enumerate(outs):
        target = jnp.bitwise_xor(place, d)
        index = (target,) if leading else (slice(None), target)
        total = parts[0][index].astype(F32)
        for part in parts[1:]:
            total = total + part[index].astype(F32)
        out[...] = total.astype(out.dtype)


def split_stage(axis, unit, parts, outer, group, own_rows, leading=False):
    columns = parts[0].shape[-1]
    shape = (*((group, outer) if leading else (outer, group)), own_rows, columns)
    made = (outer, own_rows, columns)
    return pl.pallas_call(
        functools.partial(split_kernel, group, leading, axis, unit),
        out_shape=[jax.ShapeDtypeStruct(made, F32 if d == 0 else BF16) for d in range(group)],
        in_specs=[VMEM] * len(parts),
        out_specs=[VMEM] * group,
        cost_estimate=cost(outer * group * own_rows * columns * 1000),
        compiler_params=PARAMS,
    )(*[part.reshape(shape) for part in parts])


def swap(array, axis, distance):
    count = lax.axis_size(axis)
    return lax.ppermute(array, axis, [(i, i ^ distance) for i in range(count)])


def exchange(parts, axis, unit):
    return [parts[0]] + [swap(parts[d], axis, d * unit) for d in range(1, len(parts))]


def on_device(inputs, first_weight, second_weight, targets, noise_var, assignment):
    gx_count = lax.axis_size("gx")
    gy_count = lax.axis_size("gy")
    devices = gx_count * gy_count
    per_slot = CAP // devices
    rows, din = inputs.shape
    hid, feat = second_weight.shape
    own_rows = din // devices
    if tight(devices):
        sent_shape = packed_shape = (devices, din // 128 * per_slot + per_slot // 2, 128)
    else:
        sent_shape, packed_shape = (CAP, din + 128), (devices, per_slot, din + 128)
    sent = pl.pallas_call(
        functools.partial(dispatch_kernel, devices),
        out_shape=jax.ShapeDtypeStruct(sent_shape, BF16),
        in_specs=[HBM] * 3,
        out_specs=VMEM,
        scratch_shapes=[
            pltpu.VMEM((1, rows), jnp.int32),
            pltpu.VMEM((rows,), BF16),
            pltpu.VMEM((rows, din), BF16),
            pltpu.SemaphoreType.DMA((3,)),
        ],
        cost_estimate=cost(2 * CAP * rows * din),
    )(assignment.reshape(1, rows), targets, inputs)
    got = lax.all_to_all(
        sent.reshape(packed_shape), ("gx", "gy"), split_axis=0, concat_axis=0, tiled=True
    ).reshape(sent_shape)

    half = din // 2
    x, targ, xt = pl.pallas_call(
        functools.partial(unpack_kernel, devices),
        out_shape=[
            jax.ShapeDtypeStruct((CAP, din), BF16),
            jax.ShapeDtypeStruct((CAP, 128), F32),
            jax.ShapeDtypeStruct((2, half, CAP), BF16),
        ],
        in_specs=[VMEM],
        out_specs=[VMEM] * 3,
        cost_estimate=cost(2 * CAP * din * hid),
        compiler_params=PARAMS,
    )(got)
    pre, grad, ht, loss = pl.pallas_call(
        functools.partial(fit_kernel, devices),
        out_shape=[
            jax.ShapeDtypeStruct((CAP, hid), F32),
            jax.ShapeDtypeStruct((CAP, feat), BF16),
            jax.ShapeDtypeStruct((2, hid // 2, CAP), BF16),
            jax.ShapeDtypeStruct((1, 1), F32),
        ],
        in_specs=[SMEM] + [VMEM] * 4,
        out_specs=[VMEM] * 4,
        scratch_shapes=[
            pltpu.VMEM((CAP, hid), BF16),
            pltpu.VMEM((CAP, feat), BF16),
            pltpu.VMEM((CAP, CAP), F32),
            pltpu.VMEM((CAP, CAP), F32),
        ],
        cost_estimate=cost(8 * CAP * din * hid),
        compiler_params=PARAMS,
    )(noise_var, x, targ, first_weight, second_weight)

    keep1, send1 = pl.pallas_call(
        first_kernel,
        out_shape=[jax.ShapeDtypeStruct((half, hid), kind) for kind in (F32, BF16)],
        in_specs=[VMEM] * 4,
        out_specs=[VMEM] * 2,
        cost_estimate=cost(2 * CAP * din * hid * 4),
        compiler_params=PARAMS,
    )(grad, second_weight, pre, xt)
    keep1, ht = lax.optimization_barrier((keep1, ht))
    keep2, send2 = pl.pallas_call(
        second_kernel,
        out_shape=[jax.ShapeDtypeStruct((hid // 2, feat), kind) for kind in (F32, BF16)],
        in_specs=[VMEM] * 2,
        out_specs=[VMEM] * 2,
        cost_estimate=cost(2 * CAP * hid * feat * 2),
        compiler_params=PARAMS,
    )(grad, ht)

    plane = gy_count // 2

    def by_gy(parts, outer):
        return split_stage("gy", 2, parts, outer, plane, own_rows)

    def by_gx(parts, outer):
        return split_stage("gx", 1, parts, outer, gx_count, own_rows, True)

    def added(parts):
        return sum(part.astype(F32) for part in parts).reshape(own_rows, -1)

    first_parts = [*by_gy([keep1, swap(send1, "gy", 1)], gx_count)]
    first_parts[0], keep2 = lax.optimization_barrier((first_parts[0], keep2))
    first_parts = exchange(first_parts, "gy", 2)
    second_parts = exchange(by_gx([keep2, swap(send2, "gy", 1)], plane), "gx", 1)
    first_parts = exchange(by_gx(first_parts, 1), "gx", 1)
    first_parts[1], second_parts[0] = lax.optimization_barrier((first_parts[1], second_parts[0]))
    second_parts = exchange(by_gy(second_parts, 1), "gy", 2)
    second_total = added(second_parts)
    first_total = added(first_parts)
    return (first_total, second_total, loss.reshape(1))


def solution(mesh):
    return jax.shard_map(
        on_device,
        mesh=mesh,
        in_specs=(
            P(("gx", "gy"), None),
            P(),
            P(),
            P(("gx", "gy")),
            P(("gx", "gy")),
            P(("gx", "gy"), None),
        ),
        out_specs=(P(("gx", "gy"), None), P(("gx", "gy"), None), P(("gx", "gy"))),
        check_vma=False,
    )
```

time: 92.4 us -> 80.1 us (0.87)
  local copies, waits for them, and re-layouts: 6.25 us -> 0.82 us
  Pallas kernels: 17.7 us -> 12.6 us
  starting transfers between devices: 23.9 us -> 22 us
    unnamed x16 -> x4, local copies, waits for them, and re-layouts: 6.25 us -> 0.82 us
    pallas_call x1, Pallas kernels: 8.8 us -> 5.94 us  [on_device(): pl.pallas_call(functools.partial(fit_kernel, devices), out_shape=[jax.Sha...]
    ppermute x14, starting transfers between devices: 16.6 us -> 14.7 us  [swap(): return lax.ppermute(array, axis, [(i, i ^ distance) for i in range(count)])]
    pallas_call x1, Pallas kernels: 4.11 us -> 2.57 us  [on_device(): pl.pallas_call(first_kernel, out_shape=[jax.ShapeDtypeStruct((half, hid),...]
    pallas_call x5 -> x6, Pallas kernels: 2.83 us -> 1.55 us  [the longest x1 0.71 us: on_device(): pl.pallas_call(second_kernel, out_shape=[jax.ShapeDtypeStruct((hid // 2,...]
  transfers between devices with their start and end apart: 15 -> 15, of which waited for: 4 -> 8; matrix products, arithmetic and copies ran while one was open for 1% -> 1% of each run, Pallas kernels for 7% -> 1%
where the time goes in v2:
time: 80.1 us; the launch traced here: 79.8 us
  waiting for transfers between devices  41.5 us (52%)
  starting transfers between devices  22 us (27%)
  Pallas kernels  12.6 us (16%)
  between operations  1.53 us (2%)
  other arithmetic  1.33 us (2%)
  local copies, waits for them, and re-layouts  0.82 us (1%)
    all_to_all x1, waiting for transfers between devices, on_device(): lax.all_to_all(sent.reshape(packed_shape), ('gx', 'gy'), split_axis=0, co...  26.8 us
    ppermute x14, waiting for transfers between devices, swap(): return lax.ppermute(array, axis, [(i, i ^ distance) for i in range(count)])  14.7 us
    ppermute x14, starting transfers between devices, swap(): return lax.ppermute(array, axis, [(i, i ^ distance) for i in range(count)])  14.7 us
    all_to_all x1, starting transfers between devices, on_device(): lax.all_to_all(sent.reshape(packed_shape), ('gx', 'gy'), split_axis=0, co...  7.3 us
    pallas_call x1, Pallas kernels, on_device(): pl.pallas_call(functools.partial(fit_kernel, devices), out_shape=[jax.Sha...  5.94 us
    pallas_call x1, Pallas kernels, on_device(): pl.pallas_call(functools.partial(dispatch_kernel, devices), out_shape=jax...  2.58 us
    pallas_call x1, Pallas kernels, on_device(): pl.pallas_call(first_kernel, out_shape=[jax.ShapeDtypeStruct((half, hid),...  2.57 us
  transfers between devices with their start and end apart: 15, of which 8 were waited for; matrix products, arithmetic and copies ran while one was open for 1% of the time, Pallas kernels for 1%

profile of v2, /device:TPU:0, one launch (start us, length us, event | category | flops | bytes accessed | tf_op | source)
XLA Modules:
  0.0 79.8 jit_solution(15463886315496419128)
XLA Ops:
  0.6 2.6 %shard_map.85 = bf16[32,136,128]{2,1,0:T(8,128)(2,1)} custom-call(s32[1,256]{1,0:T(1,128)} %bitcast.30, bf16[256]{0:T(256)(128)(2,1)} %targ_hbm.1, bf16[256,1024]{1,0:T(8,128)(2,1)} %rows_hbm.1), custom_call_target="tpu_custom_call" | custom-call | flops 268435456 | tf_op jit(solution)/shard_map/pallas_call | solution.py:255
  3.2 7.3 %all-to-all-start = ((bf16[32,136,128]{2,1,0:T(8,128)(2,1)}), bf16[32,136,128]{2,1,0:T(8,128)(2,1)S(1)}, u32[]{:S(2)}, u32[]{:S(2)}) async-start(bf16[32,136,128]{2,1,0:T(8,128)(2,1)} %shard_map.85), calls=%async_computation | async-start | bytes 2228224 | tf_op jit(solution)/shard_map/all_to_all | solution.py:268
  10.5 0.0 copy-start
  11.3 26.8 %all-to-all-done.got_ref = bf16[32,136,128]{2,1,0:T(8,128)(2,1)S(1)} async-done(((bf16[32,136,128]{2,1,0:T(8,128)(2,1)}), bf16[32,136,128]{2,1,0:T(8,128)(2,1)S(1)}, u32[]{:S(2)}, u32[]{:S(2)}) %all-to-all-start) | async-done | bytes 1114144 | tf_op jit(solution)/shard_map/all_to_all | solution.py:268
  38.2 0.0 copy-start.1
  38.2 0.4 shard_map.86
  38.6 0.0 copy-done
  38.6 0.8 %copy-done.1 = bf16[1024,512]{1,0:T(8,128)(2,1)S(1)} copy-done((bf16[1024,512]{1,0:T(8,128)(2,1)S(1)}, bf16[1024,512]{1,0:T(8,128)(2,1)}, u32[]{:S(2)}) %copy-start.1) | copy-done | bytes 1048600
  39.4 5.9 %shard_map.87 = (f32[512,1024]{1,0:T(8,128)S(1)}, bf16[512,512]{1,0:T(8,128)(2,1)S(1)}, bf16[2,512,512]{2,1,0:T(8,128)(2,1)S(1)}, f32[1,1]{1,0:T(1,128)}) custom-call(f32[1]{0:T(128)S(6)} %copy.9.noise_ref, bf16[512,1024]{1,0:T(8,128)(2,1)S(1)} %get-tuple-element.36.x_ref, f32[512,128]{1,0:T(8,128)S(1)} %get-tuple-element.37.targ_ref, ...), custom_call_target="tpu_custom_call" | custom-call | flops 4294967296 | tf_op jit(solution)/shard_map/pallas_call | solution.py:285
  45.3 2.6 %shard_map.88 = (f32[512,1024]{1,0:T(8,128)S(1)}, bf16[512,1024]{1,0:T(8,128)(2,1)S(1)}) custom-call(bf16[512,512]{1,0:T(8,128)(2,1)S(1)} %get-tuple-element.38.grad_ref, bf16[1024,512]{1,0:T(8,128)(2,1)S(1)} %copy-done.1, f32[512,1024]{1,0:T(8,128)S(1)} %get-tuple-element.39.pre_ref, bf16[2,512,512]{2,1,0:T(8,128)(2,1)S(1)} %get-tuple-element.40.xt_ref), custom_call_target="tpu_custom_call" | custom-call | flops 4294967296 | tf_op jit(solution)/shard_map/pallas_call | solution.py:305
  47.9 0.1 collective-permute-start
  48.0 0.7 shard_map.90
  48.7 0.6 collective-permute-start.5
  49.3 1.4 %collective-permute-done = bf16[512,1024]{1,0:T(8,128)(2,1)S(1)} collective-permute-done((bf16[512,1024]{1,0:T(8,128)(2,1)S(1)}, bf16[512,1024]{1,0:T(8,128)(2,1)S(1)}, u32[]{:S(2)}, u32[]{:S(2)}) %collective-permute-start) | collective-permute-done | bytes 1048608 | tf_op jit(solution)/shard_map/ppermute | solution.py:236
  50.6 0.2 shard_map.89
  50.8 1.5 %collective-permute-start.1 = (bf16[4,32,1024]{2,1,0:T(8,128)(2,1)S(1)}, bf16[4,32,1024]{2,1,0:T(8,128)(2,1)S(1)}, u32[]{:S(2)}, u32[]{:S(2)}) collective-permute-start(bf16[4,32,1024]{2,1,0:T(8,128)(2,1)S(1)} %get-tuple-element.49), channel_id=1, source_target_pairs={{0,2},{1,3},{2,0},{3,1},{4,6},{5,7},{6,4},{7,5},{8,10},{9,11},{10,... | collective-permute-start | bytes 786440 | tf_op jit(solution)/shard_map/ppermute | solution.py:236
  52.3 1.5 %collective-permute-start.2 = (bf16[4,32,1024]{2,1,0:T(8,128)(2,1)S(1)}, bf16[4,32,1024]{2,1,0:T(8,128)(2,1)S(1)}, u32[]{:S(2)}, u32[]{:S(2)}) collective-permute-start(bf16[4,32,1024]{2,1,0:T(8,128)(2,1)S(1)} %get-tuple-element.50), channel_id=1, source_target_pairs={{0,4},{1,5},{2,6},{3,7},{4,0},{5,1},{6,2},{7,3},{8,12},{9,13},{10,... | collective-permute-start | bytes 786440 | tf_op jit(solution)/shard_map/ppermute | solution.py:236
  53.8 0.5 collective-permute-start.3
  54.4 0.0 collective-permute-done.5
  54.4 0.1 shard_map.92
  54.5 0.7 collective-permute-start.8
  55.2 1.2 %collective-permute-start.9 = (bf16[4,32,512]{2,1,0:T(8,128)(2,1)S(1)}, bf16[4,32,512]{2,1,0:T(8,128)(2,1)S(1)}, u32[]{:S(2)}, u32[]{:S(2)}) collective-permute-start(bf16[4,32,512]{2,1,0:T(8,128)(2,1)S(1)} %get-tuple-element.62), channel_id=1, source_target_pairs={{0,16},{8,24},{16,0},{24,8},{1,17},{9,25},{17,1},{25,9},{2,18},{10... | collective-permute-start | bytes 393224 | tf_op jit(solution)/shard_map/ppermute | solution.py:236
  56.4 3.6 %collective-permute-done.1 = bf16[4,32,1024]{2,1,0:T(8,128)(2,1)S(1)} collective-permute-done((bf16[4,32,1024]{2,1,0:T(8,128)(2,1)S(1)}, bf16[4,32,1024]{2,1,0:T(8,128)(2,1)S(1)}, u32[]{:S(2)}, u32[]{:S(2)}) %collective-permute-start.1) | collective-permute-done | bytes 262176 | tf_op jit(solution)/shard_map/ppermute | solution.py:236
  60.0 1.3 %collective-permute-start.10 = (bf16[4,32,512]{2,1,0:T(8,128)(2,1)S(1)}, bf16[4,32,512]{2,1,0:T(8,128)(2,1)S(1)}, u32[]{:S(2)}, u32[]{:S(2)}) collective-permute-start(bf16[4,32,512]{2,1,0:T(8,128)(2,1)S(1)} %get-tuple-element.63), channel_id=1, source_target_pairs={{0,24},{8,16},{16,8},{24,0},{1,25},{9,17},{17,9},{25,1},{2,26},{10... | collective-permute-start | bytes 393224 | tf_op jit(solution)/shard_map/ppermute | solution.py:236
  61.3 4.7 %collective-permute-done.2 = bf16[4,32,1024]{2,1,0:T(8,128)(2,1)S(1)} collective-permute-done((bf16[4,32,1024]{2,1,0:T(8,128)(2,1)S(1)}, bf16[4,32,1024]{2,1,0:T(8,128)(2,1)S(1)}, u32[]{:S(2)}, u32[]{:S(2)}) %collective-permute-start.2) | collective-permute-done | bytes 262176 | tf_op jit(solution)/shard_map/ppermute | solution.py:236
  66.0 0.0 collective-permute-done.3
  66.0 0.1 shard_map.91
  66.2 0.9 %collective-permute-start.4 = (bf16[1,32,1024]{2,1,0:T(8,128)(2,1)S(1)}, bf16[1,32,1024]{2,1,0:T(8,128)(2,1)S(1)}, u32[]{:S(2)}, u32[]{:S(2)}) collective-permute-start(bf16[1,32,1024]{2,1,0:T(8,128)(2,1)S(1)} %get-tuple-element.53), channel_id=1, source_target_pairs={{0,8},{8,0},{16,24},{24,16},{1,9},{9,1},{17,25},{25,17},{2,10},{10... | collective-permute-start | bytes 196616 | tf_op jit(solution)/shard_map/ppermute | solution.py:236
  67.0 1.2 %collective-permute-start.6 = (bf16[1,32,1024]{2,1,0:T(8,128)(2,1)S(1)}, bf16[1,32,1024]{2,1,0:T(8,128)(2,1)S(1)}, u32[]{:S(2)}, u32[]{:S(2)}) collective-permute-start(bf16[1,32,1024]{2,1,0:T(8,128)(2,1)S(1)} %get-tuple-element.58), channel_id=1, source_target_pairs={{0,16},{8,24},{16,0},{24,8},{1,17},{9,25},{17,1},{25,9},{2,18},{10... | collective-permute-start | bytes 196616 | tf_op jit(solution)/shard_map/ppermute | solution.py:236
  68.2 2.2 %collective-permute-done.4 = bf16[1,32,1024]{2,1,0:T(8,128)(2,1)S(1)} collective-permute-done((bf16[1,32,1024]{2,1,0:T(8,128)(2,1)S(1)}, bf16[1,32,1024]{2,1,0:T(8,128)(2,1)S(1)}, u32[]{:S(2)}, u32[]{:S(2)}) %collective-permute-start.4) | collective-permute-done | bytes 65568 | tf_op jit(solution)/shard_map/ppermute | solution.py:236
  70.5 1.6 %collective-permute-start.7 = (bf16[1,32,1024]{2,1,0:T(8,128)(2,1)S(1)}, bf16[1,32,1024]{2,1,0:T(8,128)(2,1)S(1)}, u32[]{:S(2)}, u32[]{:S(2)}) collective-permute-start(bf16[1,32,1024]{2,1,0:T(8,128)(2,1)S(1)} %get-tuple-element.59), channel_id=1, source_target_pairs={{0,24},{8,16},{16,8},{24,0},{1,25},{9,17},{17,9},{25,1},{2,26},{10... | collective-permute-start | bytes 196616 | tf_op jit(solution)/shard_map/ppermute | solution.py:236
  72.1 0.0 collective-permute-done.8
  72.1 0.0 collective-permute-done.9
  72.1 0.0 collective-permute-done.10
  72.1 0.1 shard_map.93
  72.2 1.4 %collective-permute-start.11 = (bf16[1,32,512]{2,1,0:T(8,128)(2,1)S(1)}, bf16[1,32,512]{2,1,0:T(8,128)(2,1)S(1)}, u32[]{:S(2)}, u32[]{:S(2)}) collective-permute-start(bf16[1,32,512]{2,1,0:T(8,128)(2,1)S(1)} %get-tuple-element.65), channel_id=1, source_target_pairs={{0,2},{1,3},{2,0},{3,1},{4,6},{5,7},{6,4},{7,5},{8,10},{9,11},{10,... | collective-permute-start | bytes 98312 | tf_op jit(solution)/shard_map/ppermute | solution.py:236
  73.6 0.7 collective-permute-start.12
  74.3 1.4 %collective-permute-start.13 = (bf16[1,32,512]{2,1,0:T(8,128)(2,1)S(1)}, bf16[1,32,512]{2,1,0:T(8,128)(2,1)S(1)}, u32[]{:S(2)}, u32[]{:S(2)}) collective-permute-start(bf16[1,32,512]{2,1,0:T(8,128)(2,1)S(1)} %get-tuple-element.67), channel_id=1, source_target_pairs={{0,6},{1,7},{2,4},{3,5},{4,2},{5,3},{6,0},{7,1},{8,14},{9,15},{10,... | collective-permute-start | bytes 98312 | tf_op jit(solution)/shard_map/ppermute | solution.py:236
  75.8 0.0 collective-permute-done.6
  75.8 0.8 collective-permute-done.7
  76.5 0.7 add_bitcast_fusion
  77.2 0.0 collective-permute-done.11
  77.2 0.3 collective-permute-done.12
  77.5 1.6 %collective-permute-done.13 = bf16[1,32,512]{2,1,0:T(8,128)(2,1)S(1)} collective-permute-done((bf16[1,32,512]{2,1,0:T(8,128)(2,1)S(1)}, bf16[1,32,512]{2,1,0:T(8,128)(2,1)S(1)}, u32[]{:S(2)}, u32[]{:S(2)}) %collective-permute-start.13) | collective-permute-done | bytes 32800 | tf_op jit(solution)/shard_map/ppermute | solution.py:236
  79.1 0.6 add_bitcast_fusion.1
Async XLA Ops:
  3.2 35.0 %all-to-all-start = ((bf16[32,136,128]{2,1,0:T(8,128)(2,1)}), bf16[32,136,128]{2,1,0:T(8,128)(2,1)S(1)}, u32[]{:S(2)}, u32[]{:S(2)}) async-start(bf16[32,136,128]{2,1,0:T(8,128)(2,1)} %shard_map.85), calls=%async_computation | async-start | bytes 2228224 | tf_op jit(solution)/shard_map/all_to_all | solution.py:268
  10.5 28.1 %copy-start = (bf16[1024,1024]{1,0:T(8,128)(2,1)S(1)}, bf16[1024,1024]{1,0:T(8,128)(2,1)}, u32[]{:S(2)}) copy-start(bf16[1024,1024]{1,0:T(8,128)(2,1)} %first_ref.1) | copy-start | bytes 6291460
  38.2 1.2 %copy-start.1 = (bf16[1024,512]{1,0:T(8,128)(2,1)S(1)}, bf16[1024,512]{1,0:T(8,128)(2,1)}, u32[]{:S(2)}) copy-start(bf16[1024,512]{1,0:T(8,128)(2,1)} %second_ref.3) | copy-start | bytes 3145732
  47.9 2.7 %collective-permute-start = (bf16[512,1024]{1,0:T(8,128)(2,1)S(1)}, bf16[512,1024]{1,0:T(8,128)(2,1)S(1)}, u32[]{:S(2)}, u32[]{:S(2)}) collective-permute-start(bf16[512,1024]{1,0:T(8,128)(2,1)S(1)} %get-tuple-element.44), channel_id=1, source_target_pairs={{0,1},{1,0},{2,3},{3,2},{4,5},{5,4},{6,7},{7,6},{8,9},{9,8},{10,11... | collective-permute-start | bytes 3145736 | tf_op jit(solution)/shard_map/ppermute | solution.py:236
  48.7 5.7 %collective-permute-start.5 = (bf16[512,512]{1,0:T(8,128)(2,1)S(1)}, bf16[512,512]{1,0:T(8,128)(2,1)S(1)}, u32[]{:S(2)}, u32[]{:S(2)}) collective-permute-start(bf16[512,512]{1,0:T(8,128)(2,1)S(1)} %get-tuple-element.55), channel_id=1, source_target_pairs={{0,1},{1,0},{2,3},{3,2},{4,5},{5,4},{6,7},{7,6},{8,9},{9,8},{10,11... | collective-permute-start | bytes 1572872 | tf_op jit(solution)/shard_map/ppermute | solution.py:236
  50.8 9.2 %collective-permute-start.1 = (bf16[4,32,1024]{2,1,0:T(8,128)(2,1)S(1)}, bf16[4,32,1024]{2,1,0:T(8,128)(2,1)S(1)}, u32[]{:S(2)}, u32[]{:S(2)}) collective-permute-start(bf16[4,32,1024]{2,1,0:T(8,128)(2,1)S(1)} %get-tuple-element.49), channel_id=1, source_target_pairs={{0,2},{1,3},{2,0},{3,1},{4,6},{5,7},{6,4},{7,5},{8,10},{9,11},{10,... | collective-permute-start | bytes 786440 | tf_op jit(solution)/shard_map/ppermute | solution.py:236
  52.3 13.7 %collective-permute-start.2 = (bf16[4,32,1024]{2,1,0:T(8,128)(2,1)S(1)}, bf16[4,32,1024]{2,1,0:T(8,128)(2,1)S(1)}, u32[]{:S(2)}, u32[]{:S(2)}) collective-permute-start(bf16[4,32,1024]{2,1,0:T(8,128)(2,1)S(1)} %get-tuple-element.50), channel_id=1, source_target_pairs={{0,4},{1,5},{2,6},{3,7},{4,0},{5,1},{6,2},{7,3},{8,12},{9,13},{10,... | collective-permute-start | bytes 786440 | tf_op jit(solution)/shard_map/ppermute | solution.py:236
  53.8 12.2 %collective-permute-start.3 = (bf16[4,32,1024]{2,1,0:T(8,128)(2,1)S(1)}, bf16[4,32,1024]{2,1,0:T(8,128)(2,1)S(1)}, u32[]{:S(2)}, u32[]{:S(2)}) collective-permute-start(bf16[4,32,1024]{2,1,0:T(8,128)(2,1)S(1)} %get-tuple-element.51), channel_id=1, source_target_pairs={{0,6},{1,7},{2,4},{3,5},{4,2},{5,3},{6,0},{7,1},{8,14},{9,15},{10,... | collective-permute-start | bytes 786440 | tf_op jit(solution)/shard_map/ppermute | solution.py:236
  54.5 17.6 %collective-permute-start.8 = (bf16[4,32,512]{2,1,0:T(8,128)(2,1)S(1)}, bf16[4,32,512]{2,1,0:T(8,128)(2,1)S(1)}, u32[]{:S(2)}, u32[]{:S(2)}) collective-permute-start(bf16[4,32,512]{2,1,0:T(8,128)(2,1)S(1)} %get-tuple-element.61), channel_id=1, source_target_pairs={{0,8},{8,0},{16,24},{24,16},{1,9},{9,1},{17,25},{25,17},{2,10},{10... | collective-permute-start | bytes 393224 | tf_op jit(solution)/shard_map/ppermute | solution.py:236
  55.2 17.0 %collective-permute-start.9 = (bf16[4,32,512]{2,1,0:T(8,128)(2,1)S(1)}, bf16[4,32,512]{2,1,0:T(8,128)(2,1)S(1)}, u32[]{:S(2)}, u32[]{:S(2)}) collective-permute-start(bf16[4,32,512]{2,1,0:T(8,128)(2,1)S(1)} %get-tuple-element.62), channel_id=1, source_target_pairs={{0,16},{8,24},{16,0},{24,8},{1,17},{9,25},{17,1},{25,9},{2,18},{10... | collective-permute-start | bytes 393224 | tf_op jit(solution)/shard_map/ppermute | solution.py:236
  60.0 12.1 %collective-permute-start.10 = (bf16[4,32,512]{2,1,0:T(8,128)(2,1)S(1)}, bf16[4,32,512]{2,1,0:T(8,128)(2,1)S(1)}, u32[]{:S(2)}, u32[]{:S(2)}) collective-permute-start(bf16[4,32,512]{2,1,0:T(8,128)(2,1)S(1)} %get-tuple-element.63), channel_id=1, source_target_pairs={{0,24},{8,16},{16,8},{24,0},{1,25},{9,17},{17,9},{25,1},{2,26},{10... | collective-permute-start | bytes 393224 | tf_op jit(solution)/shard_map/ppermute | solution.py:236
  66.2 4.3 %collective-permute-start.4 = (bf16[1,32,1024]{2,1,0:T(8,128)(2,1)S(1)}, bf16[1,32,1024]{2,1,0:T(8,128)(2,1)S(1)}, u32[]{:S(2)}, u32[]{:S(2)}) collective-permute-start(bf16[1,32,1024]{2,1,0:T(8,128)(2,1)S(1)} %get-tuple-element.53), channel_id=1, source_target_pairs={{0,8},{8,0},{16,24},{24,16},{1,9},{9,1},{17,25},{25,17},{2,10},{10... | collective-permute-start | bytes 196616 | tf_op jit(solution)/shard_map/ppermute | solution.py:236
  67.0 8.7 %collective-permute-start.6 = (bf16[1,32,1024]{2,1,0:T(8,128)(2,1)S(1)}, bf16[1,32,1024]{2,1,0:T(8,128)(2,1)S(1)}, u32[]{:S(2)}, u32[]{:S(2)}) collective-permute-start(bf16[1,32,1024]{2,1,0:T(8,128)(2,1)S(1)} %get-tuple-element.58), channel_id=1, source_target_pairs={{0,16},{8,24},{16,0},{24,8},{1,17},{9,25},{17,1},{25,9},{2,18},{10... | collective-permute-start | bytes 196616 | tf_op jit(solution)/shard_map/ppermute | solution.py:236
  70.5 6.1 %collective-permute-start.7 = (bf16[1,32,1024]{2,1,0:T(8,128)(2,1)S(1)}, bf16[1,32,1024]{2,1,0:T(8,128)(2,1)S(1)}, u32[]{:S(2)}, u32[]{:S(2)}) collective-permute-start(bf16[1,32,1024]{2,1,0:T(8,128)(2,1)S(1)} %get-tuple-element.59), channel_id=1, source_target_pairs={{0,24},{8,16},{16,8},{24,0},{1,25},{9,17},{17,9},{25,1},{2,26},{10... | collective-permute-start | bytes 196616 | tf_op jit(solution)/shard_map/ppermute | solution.py:236
  72.2 5.0 %collective-permute-start.11 = (bf16[1,32,512]{2,1,0:T(8,128)(2,1)S(1)}, bf16[1,32,512]{2,1,0:T(8,128)(2,1)S(1)}, u32[]{:S(2)}, u32[]{:S(2)}) collective-permute-start(bf16[1,32,512]{2,1,0:T(8,128)(2,1)S(1)} %get-tuple-element.65), channel_id=1, source_target_pairs={{0,2},{1,3},{2,0},{3,1},{4,6},{5,7},{6,4},{7,5},{8,10},{9,11},{10,... | collective-permute-start | bytes 98312 | tf_op jit(solution)/shard_map/ppermute | solution.py:236
  73.6 3.9 %collective-permute-start.12 = (bf16[1,32,512]{2,1,0:T(8,128)(2,1)S(1)}, bf16[1,32,512]{2,1,0:T(8,128)(2,1)S(1)}, u32[]{:S(2)}, u32[]{:S(2)}) collective-permute-start(bf16[1,32,512]{2,1,0:T(8,128)(2,1)S(1)} %get-tuple-element.66), channel_id=1, source_target_pairs={{0,4},{1,5},{2,6},{3,7},{4,0},{5,1},{6,2},{7,3},{8,12},{9,13},{10,... | collective-permute-start | bytes 98312 | tf_op jit(solution)/shard_map/ppermute | solution.py:236
  74.3 4.8 %collective-permute-start.13 = (bf16[1,32,512]{2,1,0:T(8,128)(2,1)S(1)}, bf16[1,32,512]{2,1,0:T(8,128)(2,1)S(1)}, u32[]{:S(2)}, u32[]{:S(2)}) collective-permute-start(bf16[1,32,512]{2,1,0:T(8,128)(2,1)S(1)} %get-tuple-element.67), channel_id=1, source_target_pairs={{0,6},{1,7},{2,4},{3,5},{4,2},{5,3},{6,0},{7,1},{8,14},{9,15},{10,... | collective-permute-start | bytes 98312 | tf_op jit(solution)/shard_map/ppermute | solution.py:236

commit v3 on v2

--- a/solution.py
+++ b/solution.py
@@ -11,7 +11,6 @@
 POWERS = 16
 BF16 = jnp.bfloat16
 F32 = jnp.float32
-EXACT = lax.Precision.HIGHEST
 VMEM = pl.BlockSpec(memory_space=pltpu.VMEM)
 SMEM = pl.BlockSpec(memory_space=pltpu.SMEM)
 HBM = pl.BlockSpec(memory_space=pltpu.HBM)
@@ -22,13 +21,12 @@
     return pl.CostEstimate(flops=int(work), bytes_accessed=0, transcendentals=0)
 
 
-def dot(left, right, left_dim=1, right_dim=0, precision=None):
+def dot(left, right, left_dim=1, right_dim=0):
     return lax.dot_general(
         left,
         right,
         (((left_dim,), (right_dim,)), ((), ())),
         preferred_element_type=F32,
-        precision=precision,
     )
 
 
@@ -101,6 +99,14 @@
     target[1] = turned[:, 1].reshape(width // 2, CAP)
 
 
+def pieces(array, count):
+    made = []
+    for _ in range(count):
+        made.append(array.astype(BF16))
+        array = array - made[-1].astype(F32)
+    return made
+
+
 def row_to_column(gram, row):
     parts = []
     for start in range(0, CAP, 64):
@@ -118,32 +124,19 @@
     return jnp.sum(total, axis=0, keepdims=True)
 
 
-def fit_kernel(
-    blocks,
-    noise_ref,
-    x_ref,
-    targ_ref,
-    first_ref,
-    second_ref,
-    pre_ref,
-    grad_ref,
-    ht_ref,
-    loss_ref,
-    hid_ref,
-    feat_ref,
-    gram_ref,
-    resid_ref,
-):
-    hid = first_ref.shape[1]
-    feat = second_ref.shape[1]
+def hidden_kernel(x_ref, first_ref, pre_ref, hid_ref):
     step = 256
-    for i in range(0, hid, step):
+    for i in range(0, first_ref.shape[1], step):
         pre = dot(x_ref[...], first_ref[:, i : i + step])
         pre_ref[:, i : i + step] = pre
         hid_ref[:, i : i + step] = (pre * jax.nn.sigmoid(pre)).astype(BF16)
+
+
+def fit_kernel(noise_ref, hid_ref, targ_ref, second_ref, grad_ref, loss_ref, feat_ref, gram_ref, resid_ref):
+    feat = second_ref.shape[1]
+    step = 256
     for i in range(0, feat, step):
         feat_ref[:, i : i + step] = dot(hid_ref[...], second_ref[:, i : i + step]).astype(BF16)
-    split_parity(blocks, hid_ref[...], ht_ref)
 
     feats = feat_ref[...]
     gram_ref[...] = dot(feats, feats, 1, 1) * (1.0 / feat)
@@ -178,22 +171,30 @@
     moments = jnp.sum(powers * targ_row, axis=1, keepdims=True)
     last = jnp.sum(powers[7:8, :] * powers[8:9, :], axis=1, keepdims=True)
     loss_ref[...] = 0.5 * inverse * (jnp.sum(moments, axis=0, keepdims=True) + last)
-    mask = (iota((POWERS, POWERS), 0) + iota((POWERS, POWERS), 1) <= POWERS - 2).astype(F32)
-    sums = dot(mask, powers, precision=EXACT)
-    outer = dot(powers, sums, 0, 0, precision=EXACT) + (16.0 * last / root) * gram
-    high = outer.astype(BF16)
-    low = (outer - high.astype(F32)).astype(BF16)
+    mask = (iota((POWERS, POWERS), 0) + iota((POWERS, POWERS), 1) <= POWERS - 2).astype(BF16)
+    top, middle, bottom = pieces(powers, 3)
+    stacked = jnp.concatenate([top, middle, bottom], axis=0)
+    sums = dot(jnp.concatenate([mask] * 3, axis=1), stacked)
+    sums_top, sums_middle = pieces(sums, 2)
+    outer = dot(
+        jnp.concatenate([top, middle, top], axis=0),
+        jnp.concatenate([sums_top, sums_top, sums_middle], axis=0),
+        0,
+        0,
+    )
+    high, low = pieces(outer + (16.0 * last / root) * gram, 2)
     scale = -inverse * inverse * (1.0 / feat)
     grad_ref[...] = ((dot(high, feats) + dot(low, feats)) * scale).astype(BF16)
 
 
-def second_kernel(grad_ref, ht_ref, keep_ref, send_ref):
+def second_kernel(blocks, grad_ref, hid_ref, keep_ref, send_ref, ht_ref):
+    split_parity(blocks, hid_ref[...], ht_ref)
     parity = lax.axis_index("gy") % 2
     keep_ref[...] = dot(ht_ref[parity], grad_ref[...])
     send_ref[...] = dot(ht_ref[1 - parity], grad_ref[...]).astype(BF16)
 
 
-def first_kernel(grad_ref, second_ref, pre_ref, xt_ref, keep_ref, send_ref):
+def first_send_kernel(grad_ref, second_ref, pre_ref, xt_ref, send_ref, pgrad_ref):
     step = 256
     parity = lax.axis_index("gy") % 2
     for i in range(0, pre_ref.shape[1], step):
@@ -201,13 +202,20 @@
         pre = pre_ref[:, i : i + step]
         sigma = jax.nn.sigmoid(pre)
         pre_grad = (hidden_grad * sigma * (1.0 + pre * (1.0 - sigma))).astype(BF16)
+        pgrad_ref[:, i : i + step] = pre_grad
         send_ref[:, i : i + step] = dot(xt_ref[1 - parity], pre_grad).astype(BF16)
-        keep_ref[:, i : i + step] = dot(xt_ref[parity], pre_grad)
+
+
+def first_keep_kernel(pgrad_ref, xt_ref, keep_ref):
+    step = 256
+    parity = lax.axis_index("gy") % 2
+    for i in range(0, pgrad_ref.shape[1], step):
+        keep_ref[:, i : i + step] = dot(xt_ref[parity], pgrad_ref[:, i : i + step])
 
 
 def split_kernel(group, leading, axis, unit, *refs):
     parts, outs = refs[:-group], refs[-group:]
-    place = lax.axis_index(axis) // unit
+    place = lax.axis_index(axis) // unit % group
     for d, out in enumerate(outs):
         target = jnp.bitwise_xor(place, d)
         index = (target,) if leading else (slice(None), target)
@@ -282,43 +290,60 @@
         cost_estimate=cost(2 * CAP * din * hid),
         compiler_params=PARAMS,
     )(got)
-    pre, grad, ht, loss = pl.pallas_call(
-        functools.partial(fit_kernel, devices),
+    pre, hidden = pl.pallas_call(
+        hidden_kernel,
+        out_shape=[jax.ShapeDtypeStruct((CAP, hid), kind) for kind in (F32, BF16)],
+        in_specs=[VMEM] * 2,
+        out_specs=[VMEM] * 2,
+        cost_estimate=cost(2 * CAP * din * hid),
+        compiler_params=PARAMS,
+    )(x, first_weight)
+    grad, loss = pl.pallas_call(
+        fit_kernel,
         out_shape=[
-            jax.ShapeDtypeStruct((CAP, hid), F32),
             jax.ShapeDtypeStruct((CAP, feat), BF16),
-            jax.ShapeDtypeStruct((2, hid // 2, CAP), BF16),
             jax.ShapeDtypeStruct((1, 1), F32),
         ],
-        in_specs=[SMEM] + [VMEM] * 4,
-        out_specs=[VMEM] * 4,
+        in_specs=[SMEM] + [VMEM] * 3,
+        out_specs=[VMEM] * 2,
         scratch_shapes=[
-            pltpu.VMEM((CAP, hid), BF16),
             pltpu.VMEM((CAP, feat), BF16),
             pltpu.VMEM((CAP, CAP), F32),
             pltpu.VMEM((CAP, CAP), F32),
         ],
-        cost_estimate=cost(8 * CAP * din * hid),
-        compiler_params=PARAMS,
-    )(noise_var, x, targ, first_weight, second_weight)
-
-    keep1, send1 = pl.pallas_call(
-        first_kernel,
-        out_shape=[jax.ShapeDtypeStruct((half, hid), kind) for kind in (F32, BF16)],
+        cost_estimate=cost(6 * CAP * din * hid),
+        compiler_params=PARAMS,
+    )(noise_var, hidden, targ, second_weight)
+
+    send1, pre_grad = pl.pallas_call(
+        first_send_kernel,
+        out_shape=[
+            jax.ShapeDtypeStruct((half, hid), BF16),
+            jax.ShapeDtypeStruct((CAP, hid), BF16),
+        ],
         in_specs=[VMEM] * 4,
         out_specs=[VMEM] * 2,
-        cost_estimate=cost(2 * CAP * din * hid * 4),
+        cost_estimate=cost(2 * CAP * din * hid * 3),
         compiler_params=PARAMS,
     )(grad, second_weight, pre, xt)
-    keep1, ht = lax.optimization_barrier((keep1, ht))
+    keep1 = pl.pallas_call(
+        first_keep_kernel,
+        out_shape=jax.ShapeDtypeStruct((half, hid), F32),
+        in_specs=[VMEM] * 2,
+        out_specs=VMEM,
+        cost_estimate=cost(CAP * din * hid),
+        compiler_params=PARAMS,
+    )(pre_grad, xt)
+    keep1, hidden = lax.optimization_barrier((keep1, hidden))
     keep2, send2 = pl.pallas_call(
-        second_kernel,
+        functools.partial(second_kernel, devices),
         out_shape=[jax.ShapeDtypeStruct((hid // 2, feat), kind) for kind in (F32, BF16)],
         in_specs=[VMEM] * 2,
         out_specs=[VMEM] * 2,
+        scratch_shapes=[pltpu.VMEM((2, hid // 2, CAP), BF16)],
         cost_estimate=cost(2 * CAP * hid * feat * 2),
         compiler_params=PARAMS,
-    )(grad, ht)
+    )(grad, hidden)
 
     plane = gy_count // 2
 
@@ -335,9 +360,11 @@
     first_parts[0], keep2 = lax.optimization_barrier((first_parts[0], keep2))
     first_parts = exchange(first_parts, "gy", 2)
     second_parts = exchange(by_gx([keep2, swap(send2, "gy", 1)], plane), "gx", 1)
+
+    second_parts = [*by_gy(second_parts, 1)]
     first_parts = exchange(by_gx(first_parts, 1), "gx", 1)
-    first_parts[1], second_parts[0] = lax.optimization_barrier((first_parts[1], second_parts[0]))
-    second_parts = exchange(by_gy(second_parts, 1), "gy", 2)
+    first_parts[1], *second_parts = lax.optimization_barrier((first_parts[1], *second_parts))
+    second_parts = exchange(second_parts, "gy", 2)
     second_total = added(second_parts)
     first_total = added(first_parts)
     return (first_total, second_total, loss.reshape(1))

time: 80.1 us -> 76.8 us (0.959)
  waiting for transfers between devices: 41.5 us -> 38.6 us
  local copies, waits for them, and re-layouts: 0.82 us -> 0.01 us
    ppermute x14, waiting for transfers between devices: 14.7 us -> 11.7 us  [swap(): return lax.ppermute(array, axis, [(i, i ^ distance) for i in range(count)])]
    unnamed x4, local copies, waits for them, and re-layouts: 0.82 us -> 0.01 us
    pallas_call x3 -> x5, Pallas kernels: 9.21 us -> 8.99 us  [the longest x1 4.2 us: on_device(): pl.pallas_call(fit_kernel, out_shape=[jax.ShapeDtypeStruct((CAP, feat), B...]
  transfers between devices with their start and end apart: 15 -> 15, of which waited for: 8 -> 7; matrix products, arithmetic and copies ran while one was open for 1% -> 1% of each run, Pallas kernels for 1% -> 3%
where the time goes in v3:
time: 76.8 us; the launch traced here: 76.6 us
  waiting for transfers between devices  38.6 us (50%)
  starting transfers between devices  22.7 us (30%)
  Pallas kernels  12.4 us (16%)
  between operations  1.56 us (2%)
  other arithmetic  1.33 us (2%)
    all_to_all x1, waiting for transfers between devices, on_device(): lax.all_to_all(sent.reshape(packed_shape), ('gx', 'gy'), split_axis=0, co...  26.8 us
    ppermute x14, starting transfers between devices, swap(): return lax.ppermute(array, axis, [(i, i ^ distance) for i in range(count)])  15.4 us
    ppermute x14, waiting for transfers between devices, swap(): return lax.ppermute(array, axis, [(i, i ^ distance) for i in range(count)])  11.7 us
    all_to_all x1, starting transfers between devices, on_device(): lax.all_to_all(sent.reshape(packed_shape), ('gx', 'gy'), split_axis=0, co...  7.3 us
    pallas_call x1, Pallas kernels, on_device(): pl.pallas_call(fit_kernel, out_shape=[jax.ShapeDtypeStruct((CAP, feat), B...  4.2 us
    pallas_call x1, Pallas kernels, on_device(): pl.pallas_call(functools.partial(dispatch_kernel, devices), out_shape=jax...  2.57 us
    pallas_call x1, Pallas kernels, on_device(): pl.pallas_call(first_send_kernel, out_shape=[jax.ShapeDtypeStruct((half,...  1.92 us
  transfers between devices with their start and end apart: 15, of which 7 were waited for; matrix products, arithmetic and copies ran while one was open for 1% of the time, Pallas kernels for 3%

profile of v3, /device:TPU:0, one launch (start us, length us, event | category | flops | bytes accessed | tf_op | source)
XLA Modules:
  0.0 76.6 jit_solution(2848335661993161465)
XLA Ops:
  0.6 2.6 %shard_map.85 = bf16[32,136,128]{2,1,0:T(8,128)(2,1)} custom-call(s32[1,256]{1,0:T(1,128)} %bitcast.30, bf16[256]{0:T(256)(128)(2,1)} %targ_hbm.1, bf16[256,1024]{1,0:T(8,128)(2,1)} %rows_hbm.1), custom_call_target="tpu_custom_call" | custom-call | flops 268435456 | tf_op jit(solution)/shard_map/pallas_call | solution.py:263
  3.2 7.3 %all-to-all-start = ((bf16[32,136,128]{2,1,0:T(8,128)(2,1)}), bf16[32,136,128]{2,1,0:T(8,128)(2,1)S(1)}, u32[]{:S(2)}, u32[]{:S(2)}) async-start(bf16[32,136,128]{2,1,0:T(8,128)(2,1)} %shard_map.85), calls=%async_computation | async-start | bytes 2228224 | tf_op jit(solution)/shard_map/all_to_all | solution.py:276
  10.5 0.0 copy-start
  11.3 26.8 %all-to-all-done.got_ref = bf16[32,136,128]{2,1,0:T(8,128)(2,1)S(1)} async-done(((bf16[32,136,128]{2,1,0:T(8,128)(2,1)}), bf16[32,136,128]{2,1,0:T(8,128)(2,1)S(1)}, u32[]{:S(2)}, u32[]{:S(2)}) %all-to-all-start) | async-done | bytes 1114144 | tf_op jit(solution)/shard_map/all_to_all | solution.py:276
  38.2 0.4 shard_map.86
  38.6 0.0 copy-start.1
  38.6 0.0 copy-done
  38.6 1.3 %shard_map.87 = (f32[512,1024]{1,0:T(8,128)S(1)}, bf16[512,1024]{1,0:T(8,128)(2,1)S(1)}) custom-call(bf16[512,1024]{1,0:T(8,128)(2,1)S(1)} %get-tuple-element.39.x_ref, bf16[1024,1024]{1,0:T(8,128)(2,1)S(1)} %copy-done), custom_call_target="tpu_custom_call" | custom-call | flops 1073741824 | tf_op jit(solution)/shard_map/pallas_call | solution.py:293
  39.9 0.0 copy-done.1
  39.9 4.2 %shard_map.88 = (bf16[512,512]{1,0:T(8,128)(2,1)S(1)}, f32[1,1]{1,0:T(1,128)}) custom-call(f32[1]{0:T(128)S(6)} %copy.9.noise_ref, bf16[512,1024]{1,0:T(8,128)(2,1)S(1)} %get-tuple-element.49.hid_ref, f32[512,128]{1,0:T(8,128)S(1)} %get-tuple-element.41.targ_ref, bf16[1024,512]{1,0:T(8,128)(2,1)S(1)} %copy-done.1), custom_call_target="tpu_custom_call" | custom-call | flops 3221225472 | tf_op jit(solution)/shard_map/pallas_call | solution.py:301
  44.1 1.9 %shard_map.89 = (bf16[512,1024]{1,0:T(8,128)(2,1)S(1)}, bf16[512,1024]{1,0:T(8,128)(2,1)S(1)}) custom-call(bf16[512,512]{1,0:T(8,128)(2,1)S(1)} %get-tuple-element.42.grad_ref, bf16[1024,512]{1,0:T(8,128)(2,1)S(1)} %copy-done.1, f32[512,1024]{1,0:T(8,128)S(1)} %get-tuple-element.43.pre_ref, bf16[2,512,512]{2,1,0:T(8,128)(2,1)S(1)} %get-tuple-element.44.xt_ref), custom_call_target="tpu_custom_call" | custom-call | flops 3221225472 | tf_op jit(solution)/shard_map/pallas_call | solution.py:318
  46.0 0.1 collective-permute-start
  46.1 0.7 shard_map.90
  46.8 0.9 %shard_map.92 = (f32[512,512]{1,0:T(8,128)S(1)}, bf16[512,512]{1,0:T(8,128)(2,1)S(1)}) custom-call(bf16[512,512]{1,0:T(8,128)(2,1)S(1)} %get-tuple-element.42.grad_ref, bf16[512,1024]{1,0:T(8,128)(2,1)S(1)} %get-tuple-element.49.hid_ref), custom_call_target="tpu_custom_call" | custom-call | flops 1073741824 | tf_op jit(solution)/shard_map/pallas_call | solution.py:338
  47.7 0.6 collective-permute-start.5
  48.3 0.5 collective-permute-done
  48.7 0.2 shard_map.91
  48.9 1.5 %collective-permute-start.1 = (bf16[4,32,1024]{2,1,0:T(8,128)(2,1)S(1)}, bf16[4,32,1024]{2,1,0:T(8,128)(2,1)S(1)}, u32[]{:S(2)}, u32[]{:S(2)}) collective-permute-start(bf16[4,32,1024]{2,1,0:T(8,128)(2,1)S(1)} %get-tuple-element.52), channel_id=1, source_target_pairs={{0,2},{1,3},{2,0},{3,1},{4,6},{5,7},{6,4},{7,5},{8,10},{9,11},{10,... | collective-permute-start | bytes 786440 | tf_op jit(solution)/shard_map/ppermute | solution.py:244
  50.4 1.5 %collective-permute-start.2 = (bf16[4,32,1024]{2,1,0:T(8,128)(2,1)S(1)}, bf16[4,32,1024]{2,1,0:T(8,128)(2,1)S(1)}, u32[]{:S(2)}, u32[]{:S(2)}) collective-permute-start(bf16[4,32,1024]{2,1,0:T(8,128)(2,1)S(1)} %get-tuple-element.53), channel_id=1, source_target_pairs={{0,4},{1,5},{2,6},{3,7},{4,0},{5,1},{6,2},{7,3},{8,12},{9,13},{10,... | collective-permute-start | bytes 786440 | tf_op jit(solution)/shard_map/ppermute | solution.py:244
  51.9 0.5 collective-permute-start.3
  52.5 0.0 collective-permute-done.5
  52.5 0.1 shard_map.94
  52.6 0.7 collective-permute-start.6
  53.3 1.2 %collective-permute-start.7 = (bf16[4,32,512]{2,1,0:T(8,128)(2,1)S(1)}, bf16[4,32,512]{2,1,0:T(8,128)(2,1)S(1)}, u32[]{:S(2)}, u32[]{:S(2)}) collective-permute-start(bf16[4,32,512]{2,1,0:T(8,128)(2,1)S(1)} %get-tuple-element.61), channel_id=1, source_target_pairs={{0,16},{8,24},{16,0},{24,8},{1,17},{9,25},{17,1},{25,9},{2,18},{10... | collective-permute-start | bytes 393224 | tf_op jit(solution)/shard_map/ppermute | solution.py:244
  54.5 3.6 %collective-permute-done.1 = bf16[4,32,1024]{2,1,0:T(8,128)(2,1)S(1)} collective-permute-done((bf16[4,32,1024]{2,1,0:T(8,128)(2,1)S(1)}, bf16[4,32,1024]{2,1,0:T(8,128)(2,1)S(1)}, u32[]{:S(2)}, u32[]{:S(2)}) %collective-permute-start.1) | collective-permute-done | bytes 262176 | tf_op jit(solution)/shard_map/ppermute | solution.py:244
  58.1 1.3 %collective-permute-start.8 = (bf16[4,32,512]{2,1,0:T(8,128)(2,1)S(1)}, bf16[4,32,512]{2,1,0:T(8,128)(2,1)S(1)}, u32[]{:S(2)}, u32[]{:S(2)}) collective-permute-start(bf16[4,32,512]{2,1,0:T(8,128)(2,1)S(1)} %get-tuple-element.62), channel_id=1, source_target_pairs={{0,24},{8,16},{16,8},{24,0},{1,25},{9,17},{17,9},{25,1},{2,26},{10... | collective-permute-start | bytes 393224 | tf_op jit(solution)/shard_map/ppermute | solution.py:244
  59.4 4.7 %collective-permute-done.2 = bf16[4,32,1024]{2,1,0:T(8,128)(2,1)S(1)} collective-permute-done((bf16[4,32,1024]{2,1,0:T(8,128)(2,1)S(1)}, bf16[4,32,1024]{2,1,0:T(8,128)(2,1)S(1)}, u32[]{:S(2)}, u32[]{:S(2)}) %collective-permute-start.2) | collective-permute-done | bytes 262176 | tf_op jit(solution)/shard_map/ppermute | solution.py:244
  64.1 0.0 collective-permute-done.3
  64.1 0.1 shard_map.93
  64.3 0.9 %collective-permute-start.4 = (bf16[1,32,1024]{2,1,0:T(8,128)(2,1)S(1)}, bf16[1,32,1024]{2,1,0:T(8,128)(2,1)S(1)}, u32[]{:S(2)}, u32[]{:S(2)}) collective-permute-start(bf16[1,32,1024]{2,1,0:T(8,128)(2,1)S(1)} %get-tuple-element.56), channel_id=1, source_target_pairs={{0,8},{8,0},{16,24},{24,16},{1,9},{9,1},{17,25},{25,17},{2,10},{10... | collective-permute-start | bytes 196616 | tf_op jit(solution)/shard_map/ppermute | solution.py:244
  65.1 1.2 %collective-permute-start.9 = (bf16[1,32,1024]{2,1,0:T(8,128)(2,1)S(1)}, bf16[1,32,1024]{2,1,0:T(8,128)(2,1)S(1)}, u32[]{:S(2)}, u32[]{:S(2)}) collective-permute-start(bf16[1,32,1024]{2,1,0:T(8,128)(2,1)S(1)} %get-tuple-element.68), channel_id=1, source_target_pairs={{0,16},{8,24},{16,0},{24,8},{1,17},{9,25},{17,1},{25,9},{2,18},{10... | collective-permute-start | bytes 196616 | tf_op jit(solution)/shard_map/ppermute | solution.py:244
  66.3 0.0 collective-permute-done.6
  66.3 2.4 %collective-permute-start.10 = (bf16[1,32,1024]{2,1,0:T(8,128)(2,1)S(1)}, bf16[1,32,1024]{2,1,0:T(8,128)(2,1)S(1)}, u32[]{:S(2)}, u32[]{:S(2)}) collective-permute-start(bf16[1,32,1024]{2,1,0:T(8,128)(2,1)S(1)} %get-tuple-element.69), channel_id=1, source_target_pairs={{0,24},{8,16},{16,8},{24,0},{1,25},{9,17},{17,9},{25,1},{2,26},{10... | collective-permute-start | bytes 196616 | tf_op jit(solution)/shard_map/ppermute | solution.py:244
  68.7 0.0 collective-permute-done.7
  68.7 0.0 collective-permute-done.8
  68.7 0.1 shard_map.95
  68.8 0.0 collective-permute-done.4
  68.8 1.3 %collective-permute-start.11 = (bf16[1,32,512]{2,1,0:T(8,128)(2,1)S(1)}, bf16[1,32,512]{2,1,0:T(8,128)(2,1)S(1)}, u32[]{:S(2)}, u32[]{:S(2)}) collective-permute-start(bf16[1,32,512]{2,1,0:T(8,128)(2,1)S(1)} %get-tuple-element.71), channel_id=1, source_target_pairs={{0,2},{1,3},{2,0},{3,1},{4,6},{5,7},{6,4},{7,5},{8,10},{9,11},{10,... | collective-permute-start | bytes 98312 | tf_op jit(solution)/shard_map/ppermute | solution.py:244
  70.1 1.1 %collective-permute-start.12 = (bf16[1,32,512]{2,1,0:T(8,128)(2,1)S(1)}, bf16[1,32,512]{2,1,0:T(8,128)(2,1)S(1)}, u32[]{:S(2)}, u32[]{:S(2)}) collective-permute-start(bf16[1,32,512]{2,1,0:T(8,128)(2,1)S(1)} %get-tuple-element.72), channel_id=1, source_target_pairs={{0,4},{1,5},{2,6},{3,7},{4,0},{5,1},{6,2},{7,3},{8,12},{9,13},{10,... | collective-permute-start | bytes 98312 | tf_op jit(solution)/shard_map/ppermute | solution.py:244
  71.1 1.2 %collective-permute-start.13 = (bf16[1,32,512]{2,1,0:T(8,128)(2,1)S(1)}, bf16[1,32,512]{2,1,0:T(8,128)(2,1)S(1)}, u32[]{:S(2)}, u32[]{:S(2)}) collective-permute-start(bf16[1,32,512]{2,1,0:T(8,128)(2,1)S(1)} %get-tuple-element.73), channel_id=1, source_target_pairs={{0,6},{1,7},{2,4},{3,5},{4,2},{5,3},{6,0},{7,1},{8,14},{9,15},{10,... | collective-permute-start | bytes 98312 | tf_op jit(solution)/shard_map/ppermute | solution.py:244
  72.3 0.0 collective-permute-done.9
  72.3 0.2 collective-permute-done.10
  72.5 0.7 add_bitcast_fusion
  73.2 0.0 collective-permute-done.11
  73.2 0.8 %collective-permute-done.12 = bf16[1,32,512]{2,1,0:T(8,128)(2,1)S(1)} collective-permute-done((bf16[1,32,512]{2,1,0:T(8,128)(2,1)S(1)}, bf16[1,32,512]{2,1,0:T(8,128)(2,1)S(1)}, u32[]{:S(2)}, u32[]{:S(2)}) %collective-permute-start.12) | collective-permute-done | bytes 32800 | tf_op jit(solution)/shard_map/ppermute | solution.py:244
  74.0 2.0 %collective-permute-done.13 = bf16[1,32,512]{2,1,0:T(8,128)(2,1)S(1)} collective-permute-done((bf16[1,32,512]{2,1,0:T(8,128)(2,1)S(1)}, bf16[1,32,512]{2,1,0:T(8,128)(2,1)S(1)}, u32[]{:S(2)}, u32[]{:S(2)}) %collective-permute-start.13) | collective-permute-done | bytes 32800 | tf_op jit(solution)/shard_map/ppermute | solution.py:244
  75.9 0.6 add_bitcast_fusion.1
Async XLA Ops:
  3.2 35.0 %all-to-all-start = ((bf16[32,136,128]{2,1,0:T(8,128)(2,1)}), bf16[32,136,128]{2,1,0:T(8,128)(2,1)S(1)}, u32[]{:S(2)}, u32[]{:S(2)}) async-start(bf16[32,136,128]{2,1,0:T(8,128)(2,1)} %shard_map.85), calls=%async_computation | async-start | bytes 2228224 | tf_op jit(solution)/shard_map/all_to_all | solution.py:276
  10.5 28.1 %copy-start = (bf16[1024,1024]{1,0:T(8,128)(2,1)S(1)}, bf16[1024,1024]{1,0:T(8,128)(2,1)}, u32[]{:S(2)}) copy-start(bf16[1024,1024]{1,0:T(8,128)(2,1)} %first_ref.1) | copy-start | bytes 6291460
  38.6 1.3 %copy-start.1 = (bf16[1024,512]{1,0:T(8,128)(2,1)S(1)}, bf16[1024,512]{1,0:T(8,128)(2,1)}, u32[]{:S(2)}) copy-start(bf16[1024,512]{1,0:T(8,128)(2,1)} %second_ref.3) | copy-start | bytes 3145732
  46.0 2.7 %collective-permute-start = (bf16[512,1024]{1,0:T(8,128)(2,1)S(1)}, bf16[512,1024]{1,0:T(8,128)(2,1)S(1)}, u32[]{:S(2)}, u32[]{:S(2)}) collective-permute-start(bf16[512,1024]{1,0:T(8,128)(2,1)S(1)} %get-tuple-element.47), channel_id=1, source_target_pairs={{0,1},{1,0},{2,3},{3,2},{4,5},{5,4},{6,7},{7,6},{8,9},{9,8},{10,11... | collective-permute-start | bytes 3145736 | tf_op jit(solution)/shard_map/ppermute | solution.py:244
  47.7 4.8 %collective-permute-start.5 = (bf16[512,512]{1,0:T(8,128)(2,1)S(1)}, bf16[512,512]{1,0:T(8,128)(2,1)S(1)}, u32[]{:S(2)}, u32[]{:S(2)}) collective-permute-start(bf16[512,512]{1,0:T(8,128)(2,1)S(1)} %get-tuple-element.58), channel_id=1, source_target_pairs={{0,1},{1,0},{2,3},{3,2},{4,5},{5,4},{6,7},{7,6},{8,9},{9,8},{10,11... | collective-permute-start | bytes 1572872 | tf_op jit(solution)/shard_map/ppermute | solution.py:244
  48.9 9.2 %collective-permute-start.1 = (bf16[4,32,1024]{2,1,0:T(8,128)(2,1)S(1)}, bf16[4,32,1024]{2,1,0:T(8,128)(2,1)S(1)}, u32[]{:S(2)}, u32[]{:S(2)}) collective-permute-start(bf16[4,32,1024]{2,1,0:T(8,128)(2,1)S(1)} %get-tuple-element.52), channel_id=1, source_target_pairs={{0,2},{1,3},{2,0},{3,1},{4,6},{5,7},{6,4},{7,5},{8,10},{9,11},{10,... | collective-permute-start | bytes 786440 | tf_op jit(solution)/shard_map/ppermute | solution.py:244
  50.4 13.7 %collective-permute-start.2 = (bf16[4,32,1024]{2,1,0:T(8,128)(2,1)S(1)}, bf16[4,32,1024]{2,1,0:T(8,128)(2,1)S(1)}, u32[]{:S(2)}, u32[]{:S(2)}) collective-permute-start(bf16[4,32,1024]{2,1,0:T(8,128)(2,1)S(1)} %get-tuple-element.53), channel_id=1, source_target_pairs={{0,4},{1,5},{2,6},{3,7},{4,0},{5,1},{6,2},{7,3},{8,12},{9,13},{10,... | collective-permute-start | bytes 786440 | tf_op jit(solution)/shard_map/ppermute | solution.py:244
  51.9 12.2 %collective-permute-start.3 = (bf16[4,32,1024]{2,1,0:T(8,128)(2,1)S(1)}, bf16[4,32,1024]{2,1,0:T(8,128)(2,1)S(1)}, u32[]{:S(2)}, u32[]{:S(2)}) collective-permute-start(bf16[4,32,1024]{2,1,0:T(8,128)(2,1)S(1)} %get-tuple-element.54), channel_id=1, source_target_pairs={{0,6},{1,7},{2,4},{3,5},{4,2},{5,3},{6,0},{7,1},{8,14},{9,15},{10,... | collective-permute-start | bytes 786440 | tf_op jit(solution)/shard_map/ppermute | solution.py:244
  52.6 13.8 %collective-permute-start.6 = (bf16[4,32,512]{2,1,0:T(8,128)(2,1)S(1)}, bf16[4,32,512]{2,1,0:T(8,128)(2,1)S(1)}, u32[]{:S(2)}, u32[]{:S(2)}) collective-permute-start(bf16[4,32,512]{2,1,0:T(8,128)(2,1)S(1)} %get-tuple-element.60), channel_id=1, source_target_pairs={{0,8},{8,0},{16,24},{24,16},{1,9},{9,1},{17,25},{25,17},{2,10},{10... | collective-permute-start | bytes 393224 | tf_op jit(solution)/shard_map/ppermute | solution.py:244
  53.3 15.5 %collective-permute-start.7 = (bf16[4,32,512]{2,1,0:T(8,128)(2,1)S(1)}, bf16[4,32,512]{2,1,0:T(8,128)(2,1)S(1)}, u32[]{:S(2)}, u32[]{:S(2)}) collective-permute-start(bf16[4,32,512]{2,1,0:T(8,128)(2,1)S(1)} %get-tuple-element.61), channel_id=1, source_target_pairs={{0,16},{8,24},{16,0},{24,8},{1,17},{9,25},{17,1},{25,9},{2,18},{10... | collective-permute-start | bytes 393224 | tf_op jit(solution)/shard_map/ppermute | solution.py:244
  58.1 10.6 %collective-permute-start.8 = (bf16[4,32,512]{2,1,0:T(8,128)(2,1)S(1)}, bf16[4,32,512]{2,1,0:T(8,128)(2,1)S(1)}, u32[]{:S(2)}, u32[]{:S(2)}) collective-permute-start(bf16[4,32,512]{2,1,0:T(8,128)(2,1)S(1)} %get-tuple-element.62), channel_id=1, source_target_pairs={{0,24},{8,16},{16,8},{24,0},{1,25},{9,17},{17,9},{25,1},{2,26},{10... | collective-permute-start | bytes 393224 | tf_op jit(solution)/shard_map/ppermute | solution.py:244
  64.3 4.5 %collective-permute-start.4 = (bf16[1,32,1024]{2,1,0:T(8,128)(2,1)S(1)}, bf16[1,32,1024]{2,1,0:T(8,128)(2,1)S(1)}, u32[]{:S(2)}, u32[]{:S(2)}) collective-permute-start(bf16[1,32,1024]{2,1,0:T(8,128)(2,1)S(1)} %get-tuple-element.56), channel_id=1, source_target_pairs={{0,8},{8,0},{16,24},{24,16},{1,9},{9,1},{17,25},{25,17},{2,10},{10... | collective-permute-start | bytes 196616 | tf_op jit(solution)/shard_map/ppermute | solution.py:244
  65.1 7.2 %collective-permute-start.9 = (bf16[1,32,1024]{2,1,0:T(8,128)(2,1)S(1)}, bf16[1,32,1024]{2,1,0:T(8,128)(2,1)S(1)}, u32[]{:S(2)}, u32[]{:S(2)}) collective-permute-start(bf16[1,32,1024]{2,1,0:T(8,128)(2,1)S(1)} %get-tuple-element.68), channel_id=1, source_target_pairs={{0,16},{8,24},{16,0},{24,8},{1,17},{9,25},{17,1},{25,9},{2,18},{10... | collective-permute-start | bytes 196616 | tf_op jit(solution)/shard_map/ppermute | solution.py:244
  66.3 6.2 %collective-permute-start.10 = (bf16[1,32,1024]{2,1,0:T(8,128)(2,1)S(1)}, bf16[1,32,1024]{2,1,0:T(8,128)(2,1)S(1)}, u32[]{:S(2)}, u32[]{:S(2)}) collective-permute-start(bf16[1,32,1024]{2,1,0:T(8,128)(2,1)S(1)} %get-tuple-element.69), channel_id=1, source_target_pairs={{0,24},{8,16},{16,8},{24,0},{1,25},{9,17},{17,9},{25,1},{2,26},{10... | collective-permute-start | bytes 196616 | tf_op jit(solution)/shard_map/ppermute | solution.py:244
  68.8 4.4 %collective-permute-start.11 = (bf16[1,32,512]{2,1,0:T(8,128)(2,1)S(1)}, bf16[1,32,512]{2,1,0:T(8,128)(2,1)S(1)}, u32[]{:S(2)}, u32[]{:S(2)}) collective-permute-start(bf16[1,32,512]{2,1,0:T(8,128)(2,1)S(1)} %get-tuple-element.71), channel_id=1, source_target_pairs={{0,2},{1,3},{2,0},{3,1},{4,6},{5,7},{6,4},{7,5},{8,10},{9,11},{10,... | collective-permute-start | bytes 98312 | tf_op jit(solution)/shard_map/ppermute | solution.py:244
  70.1 3.9 %collective-permute-start.12 = (bf16[1,32,512]{2,1,0:T(8,128)(2,1)S(1)}, bf16[1,32,512]{2,1,0:T(8,128)(2,1)S(1)}, u32[]{:S(2)}, u32[]{:S(2)}) collective-permute-start(bf16[1,32,512]{2,1,0:T(8,128)(2,1)S(1)} %get-tuple-element.72), channel_id=1, source_target_pairs={{0,4},{1,5},{2,6},{3,7},{4,0},{5,1},{6,2},{7,3},{8,12},{9,13},{10,... | collective-permute-start | bytes 98312 | tf_op jit(solution)/shard_map/ppermute | solution.py:244
  71.1 4.8 %collective-permute-start.13 = (bf16[1,32,512]{2,1,0:T(8,128)(2,1)S(1)}, bf16[1,32,512]{2,1,0:T(8,128)(2,1)S(1)}, u32[]{:S(2)}, u32[]{:S(2)}) collective-permute-start(bf16[1,32,512]{2,1,0:T(8,128)(2,1)S(1)} %get-tuple-element.73), channel_id=1, source_target_pairs={{0,6},{1,7},{2,4},{3,5},{4,2},{5,3},{6,0},{7,1},{8,14},{9,15},{10,... | collective-permute-start | bytes 98312 | tf_op jit(solution)/shard_map/ppermute | solution.py:244

commit v4 on v3

--- a/solution.py
+++ b/solution.py
@@ -34,7 +34,9 @@
     return lax.broadcasted_iota(jnp.int32, shape, dim)
 
 
-def dispatch_kernel(devices, assign_hbm, targ_hbm, rows_hbm, out_ref, assign_ref, targ_ref, rows_ref, sems):
+def dispatch_kernel(
+    devices, assign_hbm, targ_hbm, rows_hbm, out_hbm, assign_ref, targ_ref, rows_ref, made_ref, sems, out_sems
+):
     copies = [
         pltpu.make_async_copy(source, target, sems.at[i])
         for i, (source, target) in enumerate(
@@ -52,23 +54,32 @@
     rank = dot(onehot.astype(BF16), earlier)
     slot = jnp.sum(jnp.where(onehot, rank, 0.0), axis=0, keepdims=True)
     place = assign * per_slot + slot.astype(jnp.int32)
-    here = iota((CAP, count), 0) == place
     copies[1].wait()
-    targ = targ_ref[...].astype(F32).reshape(1, count)
-    targ = jnp.sum(jnp.where(here, targ, 0.0), axis=1, keepdims=True)
+    targets = targ_ref[...].astype(F32).reshape(1, count)
     copies[2].wait()
-    placed = dot(here.astype(BF16), rows_ref[...]).astype(BF16)
-    if tight(devices):
-        for i in range(width // 128):
-            block = placed[:, i * 128 : (i + 1) * 128].reshape(devices, per_slot, 128)
-            out_ref[:, i * per_slot : (i + 1) * per_slot, :] = block
-        targ = targ.reshape(devices, per_slot, 1)
-        lane = iota((devices, per_slot // 2, 128), 2)
-        targ = jnp.where(lane < 64, targ[:, : per_slot // 2], targ[:, per_slot // 2 :])
-        out_ref[:, width // 128 * per_slot :, :] = targ.astype(BF16)
-    else:
-        out_ref[:, :width] = placed
-        out_ref[:, width:] = jnp.broadcast_to(targ, (CAP, 128)).astype(BF16)
+    half, share = CAP // 2, made_ref.shape[0] // 2
+    written = []
+    for h in range(2):
+        out_ref = made_ref.at[h * share : (h + 1) * share]
+        here = iota((half, count), 0) + h * half == place
+        targ = jnp.sum(jnp.where(here, targets, 0.0), axis=1, keepdims=True)
+        placed = dot(here.astype(BF16), rows_ref[...]).astype(BF16)
+        if tight(devices):
+            for i in range(width // 128):
+                block = placed[:, i * 128 : (i + 1) * 128].reshape(share, per_slot, 128)
+                out_ref[:, i * per_slot : (i + 1) * per_slot, :] = block
+            targ = targ.reshape(share, per_slot, 1)
+            lane = iota((share, per_slot // 2, 128), 2)
+            targ = jnp.where(lane < 64, targ[:, : per_slot // 2], targ[:, per_slot // 2 :])
+            out_ref[:, width // 128 * per_slot :, :] = targ.astype(BF16)
+        else:
+            out_ref[:, :width] = placed
+            out_ref[:, width:] = jnp.broadcast_to(targ, (half, 128)).astype(BF16)
+        copy = pltpu.make_async_copy(out_ref, out_hbm.at[h * share : (h + 1) * share], out_sems.at[h])
+        copy.start()
+        written.append(copy)
+    for copy in written:
+        copy.wait()
 
 
 def tight(devices):
@@ -245,7 +256,10 @@
 
 
 def exchange(parts, axis, unit):
-    return [parts[0]] + [swap(parts[d], axis, d * unit) for d in range(1, len(parts))]
+    count = len(parts)
+    hops = {d: min(d, count - d) if axis == "gx" else bin(d).count("1") for d in range(1, count)}
+    order = sorted(hops, key=hops.get, reverse=True)
+    return [parts[0]] + [swap(parts[d], axis, d * unit) for d in order]
 
 
 def on_device(inputs, first_weight, second_weight, targets, noise_var, assignment):
@@ -264,12 +278,14 @@
         functools.partial(dispatch_kernel, devices),
         out_shape=jax.ShapeDtypeStruct(sent_shape, BF16),
         in_specs=[HBM] * 3,
-        out_specs=VMEM,
+        out_specs=HBM,
         scratch_shapes=[
             pltpu.VMEM((1, rows), jnp.int32),
             pltpu.VMEM((rows,), BF16),
             pltpu.VMEM((rows, din), BF16),
+            pltpu.VMEM(sent_shape, BF16),
             pltpu.SemaphoreType.DMA((3,)),
+            pltpu.SemaphoreType.DMA((2,)),
         ],
         cost_estimate=cost(2 * CAP * rows * din),
     )(assignment.reshape(1, rows), targets, inputs)
@@ -363,7 +379,7 @@
 
     second_parts = [*by_gy(second_parts, 1)]
     first_parts = exchange(by_gx(first_parts, 1), "gx", 1)
-    first_parts[1], *second_parts = lax.optimization_barrier((first_parts[1], *second_parts))
+    first_parts[-2], *second_parts = lax.optimization_barrier((first_parts[-2], *second_parts))
     second_parts = exchange(second_parts, "gy", 2)
     second_total = added(second_parts)
     first_total = added(first_parts)

time: 76.8 us -> 76.6 us (level)
  transfers between devices with their start and end apart: 15 -> 15, of which waited for: 7 -> 9; matrix products, arithmetic and copies ran while one was open for 1% -> 1% of each run, Pallas kernels for 3% -> 3%
where the time goes in v4:
time: 76.6 us; the launch traced here: 76.4 us
  waiting for transfers between devices  38.5 us (50%)
  starting transfers between devices  22.7 us (30%)
  Pallas kernels  12.3 us (16%)
  between operations  1.55 us (2%)
  other arithmetic  1.33 us (2%)
    all_to_all x1, waiting for transfers between devices, on_device(): lax.all_to_all(sent.reshape(packed_shape), ('gx', 'gy'), split_axis=0, co...  26.8 us
    ppermute x14, starting transfers between devices, swap(): return lax.ppermute(array, axis, [(i, i ^ distance) for i in range(count)])  15.4 us
    ppermute x14, waiting for transfers between devices, swap(): return lax.ppermute(array, axis, [(i, i ^ distance) for i in range(count)])  11.7 us
    all_to_all x1, starting transfers between devices, on_device(): lax.all_to_all(sent.reshape(packed_shape), ('gx', 'gy'), split_axis=0, co...  7.3 us
    pallas_call x1, Pallas kernels, on_device(): pl.pallas_call(fit_kernel, out_shape=[jax.ShapeDtypeStruct((CAP, feat), B...  4.21 us
    pallas_call x1, Pallas kernels, on_device(): pl.pallas_call(functools.partial(dispatch_kernel, devices), out_shape=jax...  2.45 us
    pallas_call x1, Pallas kernels, on_device(): pl.pallas_call(first_send_kernel, out_shape=[jax.ShapeDtypeStruct((half,...  1.92 us
  transfers between devices with their start and end apart: 15, of which 9 were waited for; matrix products, arithmetic and copies ran while one was open for 1% of the time, Pallas kernels for 3%

profile of v4, /device:TPU:0, one launch (start us, length us, event | category | flops | bytes accessed | tf_op | source)
XLA Modules:
  0.0 76.4 jit_solution(11235097126947992926)
XLA Ops:
  0.6 2.4 %shard_map.85 = bf16[32,136,128]{2,1,0:T(8,128)(2,1)} custom-call(s32[1,256]{1,0:T(1,128)} %bitcast.30, bf16[256]{0:T(256)(128)(2,1)} %targ_hbm.1, bf16[256,1024]{1,0:T(8,128)(2,1)} %rows_hbm.1), custom_call_target="tpu_custom_call" | custom-call | flops 268435456 | tf_op jit(solution)/shard_map/pallas_call | solution.py:277
  3.1 7.3 %all-to-all-start = ((bf16[32,136,128]{2,1,0:T(8,128)(2,1)}), bf16[32,136,128]{2,1,0:T(8,128)(2,1)S(1)}, u32[]{:S(2)}, u32[]{:S(2)}) async-start(bf16[32,136,128]{2,1,0:T(8,128)(2,1)} %shard_map.85), calls=%async_computation | async-start | bytes 2228224 | tf_op jit(solution)/shard_map/all_to_all | solution.py:292
  10.4 0.0 copy-start
  11.2 26.8 %all-to-all-done.got_ref = bf16[32,136,128]{2,1,0:T(8,128)(2,1)S(1)} async-done(((bf16[32,136,128]{2,1,0:T(8,128)(2,1)}), bf16[32,136,128]{2,1,0:T(8,128)(2,1)S(1)}, u32[]{:S(2)}, u32[]{:S(2)}) %all-to-all-start) | async-done | bytes 1114144 | tf_op jit(solution)/shard_map/all_to_all | solution.py:292
  38.0 0.4 shard_map.86
  38.4 0.0 copy-start.1
  38.5 0.0 copy-done
  38.5 1.3 %shard_map.87 = (f32[512,1024]{1,0:T(8,128)S(1)}, bf16[512,1024]{1,0:T(8,128)(2,1)S(1)}) custom-call(bf16[512,1024]{1,0:T(8,128)(2,1)S(1)} %get-tuple-element.39.x_ref, bf16[1024,1024]{1,0:T(8,128)(2,1)S(1)} %copy-done), custom_call_target="tpu_custom_call" | custom-call | flops 1073741824 | tf_op jit(solution)/shard_map/pallas_call | solution.py:309
  39.7 0.0 copy-done.1
  39.7 4.2 %shard_map.88 = (bf16[512,512]{1,0:T(8,128)(2,1)S(1)}, f32[1,1]{1,0:T(1,128)}) custom-call(f32[1]{0:T(128)S(6)} %copy.9.noise_ref, bf16[512,1024]{1,0:T(8,128)(2,1)S(1)} %get-tuple-element.49.hid_ref, f32[512,128]{1,0:T(8,128)S(1)} %get-tuple-element.41.targ_ref, bf16[1024,512]{1,0:T(8,128)(2,1)S(1)} %copy-done.1), custom_call_target="tpu_custom_call" | custom-call | flops 3221225472 | tf_op jit(solution)/shard_map/pallas_call | solution.py:317
  44.0 1.9 %shard_map.89 = (bf16[512,1024]{1,0:T(8,128)(2,1)S(1)}, bf16[512,1024]{1,0:T(8,128)(2,1)S(1)}) custom-call(bf16[512,512]{1,0:T(8,128)(2,1)S(1)} %get-tuple-element.42.grad_ref, bf16[1024,512]{1,0:T(8,128)(2,1)S(1)} %copy-done.1, f32[512,1024]{1,0:T(8,128)S(1)} %get-tuple-element.43.pre_ref, bf16[2,512,512]{2,1,0:T(8,128)(2,1)S(1)} %get-tuple-element.44.xt_ref), custom_call_target="tpu_custom_call" | custom-call | flops 3221225472 | tf_op jit(solution)/shard_map/pallas_call | solution.py:334
  45.9 0.1 collective-permute-start
  46.0 0.7 shard_map.90
  46.7 0.9 %shard_map.92 = (f32[512,512]{1,0:T(8,128)S(1)}, bf16[512,512]{1,0:T(8,128)(2,1)S(1)}) custom-call(bf16[512,512]{1,0:T(8,128)(2,1)S(1)} %get-tuple-element.42.grad_ref, bf16[512,1024]{1,0:T(8,128)(2,1)S(1)} %get-tuple-element.49.hid_ref), custom_call_target="tpu_custom_call" | custom-call | flops 1073741824 | tf_op jit(solution)/shard_map/pallas_call | solution.py:354
  47.6 0.6 collective-permute-start.6
  48.1 0.5 collective-permute-done
  48.6 0.2 shard_map.91
  48.8 2.5 %collective-permute-start.1 = (bf16[4,32,1024]{2,1,0:T(8,128)(2,1)S(1)}, bf16[4,32,1024]{2,1,0:T(8,128)(2,1)S(1)}, u32[]{:S(2)}, u32[]{:S(2)}) collective-permute-start(bf16[4,32,1024]{2,1,0:T(8,128)(2,1)S(1)} %get-tuple-element.52), channel_id=1, source_target_pairs={{0,6},{1,7},{2,4},{3,5},{4,2},{5,3},{6,0},{7,1},{8,14},{9,15},{10,... | collective-permute-start | bytes 786440 | tf_op jit(solution)/shard_map/ppermute | solution.py:255
  51.2 0.5 collective-permute-start.2
  51.8 0.5 collective-permute-start.3
  52.3 0.0 collective-permute-done.6
  52.3 0.1 shard_map.94
  52.4 1.2 %collective-permute-start.7 = (bf16[4,32,512]{2,1,0:T(8,128)(2,1)S(1)}, bf16[4,32,512]{2,1,0:T(8,128)(2,1)S(1)}, u32[]{:S(2)}, u32[]{:S(2)}) collective-permute-start(bf16[4,32,512]{2,1,0:T(8,128)(2,1)S(1)} %get-tuple-element.61), channel_id=1, source_target_pairs={{0,16},{8,24},{16,0},{24,8},{1,17},{9,25},{17,1},{25,9},{2,18},{10... | collective-permute-start | bytes 393224 | tf_op jit(solution)/shard_map/ppermute | solution.py:255
  53.7 0.7 collective-permute-start.8
  54.4 4.6 %collective-permute-done.1 = bf16[4,32,1024]{2,1,0:T(8,128)(2,1)S(1)} collective-permute-done((bf16[4,32,1024]{2,1,0:T(8,128)(2,1)S(1)}, bf16[4,32,1024]{2,1,0:T(8,128)(2,1)S(1)}, u32[]{:S(2)}, u32[]{:S(2)}) %collective-permute-start.1) | collective-permute-done | bytes 262176 | tf_op jit(solution)/shard_map/ppermute | solution.py:255
  58.9 1.3 %collective-permute-start.9 = (bf16[4,32,512]{2,1,0:T(8,128)(2,1)S(1)}, bf16[4,32,512]{2,1,0:T(8,128)(2,1)S(1)}, u32[]{:S(2)}, u32[]{:S(2)}) collective-permute-start(bf16[4,32,512]{2,1,0:T(8,128)(2,1)S(1)} %get-tuple-element.63), channel_id=1, source_target_pairs={{0,24},{8,16},{16,8},{24,0},{1,25},{9,17},{17,9},{25,1},{2,26},{10... | collective-permute-start | bytes 393224 | tf_op jit(solution)/shard_map/ppermute | solution.py:255
  60.3 3.5 %collective-permute-done.2 = bf16[4,32,1024]{2,1,0:T(8,128)(2,1)S(1)} collective-permute-done((bf16[4,32,1024]{2,1,0:T(8,128)(2,1)S(1)}, bf16[4,32,1024]{2,1,0:T(8,128)(2,1)S(1)}, u32[]{:S(2)}, u32[]{:S(2)}) %collective-permute-start.2) | collective-permute-done | bytes 262176 | tf_op jit(solution)/shard_map/ppermute | solution.py:255
  63.8 0.0 collective-permute-done.3
  63.8 0.1 shard_map.93
  63.9 0.8 %collective-permute-start.5 = (bf16[1,32,1024]{2,1,0:T(8,128)(2,1)S(1)}, bf16[1,32,1024]{2,1,0:T(8,128)(2,1)S(1)}, u32[]{:S(2)}, u32[]{:S(2)}) collective-permute-start(bf16[1,32,1024]{2,1,0:T(8,128)(2,1)S(1)} %get-tuple-element.57), channel_id=1, source_target_pairs={{0,8},{8,0},{16,24},{24,16},{1,9},{9,1},{17,25},{25,17},{2,10},{10... | collective-permute-start | bytes 196616 | tf_op jit(solution)/shard_map/ppermute | solution.py:255
  64.7 1.3 %collective-permute-start.4 = (bf16[1,32,1024]{2,1,0:T(8,128)(2,1)S(1)}, bf16[1,32,1024]{2,1,0:T(8,128)(2,1)S(1)}, u32[]{:S(2)}, u32[]{:S(2)}) collective-permute-start(bf16[1,32,1024]{2,1,0:T(8,128)(2,1)S(1)} %get-tuple-element.56), channel_id=1, source_target_pairs={{0,16},{8,24},{16,0},{24,8},{1,17},{9,25},{17,1},{25,9},{2,18},{10... | collective-permute-start | bytes 196616 | tf_op jit(solution)/shard_map/ppermute | solution.py:255
  66.0 0.0 collective-permute-done.7
  66.0 2.3 %collective-permute-start.10 = (bf16[1,32,1024]{2,1,0:T(8,128)(2,1)S(1)}, bf16[1,32,1024]{2,1,0:T(8,128)(2,1)S(1)}, u32[]{:S(2)}, u32[]{:S(2)}) collective-permute-start(bf16[1,32,1024]{2,1,0:T(8,128)(2,1)S(1)} %get-tuple-element.69), channel_id=1, source_target_pairs={{0,24},{8,16},{16,8},{24,0},{1,25},{9,17},{17,9},{25,1},{2,26},{10... | collective-permute-start | bytes 196616 | tf_op jit(solution)/shard_map/ppermute | solution.py:255
  68.4 0.0 collective-permute-done.8
  68.4 0.0 collective-permute-done.9
  68.4 0.1 shard_map.95
  68.4 0.5 collective-permute-done.5
  68.9 2.5 %collective-permute-start.11 = (bf16[1,32,512]{2,1,0:T(8,128)(2,1)S(1)}, bf16[1,32,512]{2,1,0:T(8,128)(2,1)S(1)}, u32[]{:S(2)}, u32[]{:S(2)}) collective-permute-start(bf16[1,32,512]{2,1,0:T(8,128)(2,1)S(1)} %get-tuple-element.71), channel_id=1, source_target_pairs={{0,6},{1,7},{2,4},{3,5},{4,2},{5,3},{6,0},{7,1},{8,14},{9,15},{10,... | collective-permute-start | bytes 98312 | tf_op jit(solution)/shard_map/ppermute | solution.py:255
  71.4 0.4 collective-permute-start.12
  71.8 0.6 collective-permute-start.13
  72.4 0.5 collective-permute-done.4
  72.9 0.0 collective-permute-done.10
  72.9 0.7 add_bitcast_fusion
  73.6 0.2 collective-permute-done.11
  73.7 1.6 %collective-permute-done.12 = bf16[1,32,512]{2,1,0:T(8,128)(2,1)S(1)} collective-permute-done((bf16[1,32,512]{2,1,0:T(8,128)(2,1)S(1)}, bf16[1,32,512]{2,1,0:T(8,128)(2,1)S(1)}, u32[]{:S(2)}, u32[]{:S(2)}) %collective-permute-start.12) | collective-permute-done | bytes 32800 | tf_op jit(solution)/shard_map/ppermute | solution.py:255
  75.3 0.4 collective-permute-done.13
  75.7 0.6 add_bitcast_fusion.1
Async XLA Ops:
  3.1 35.0 %all-to-all-start = ((bf16[32,136,128]{2,1,0:T(8,128)(2,1)}), bf16[32,136,128]{2,1,0:T(8,128)(2,1)S(1)}, u32[]{:S(2)}, u32[]{:S(2)}) async-start(bf16[32,136,128]{2,1,0:T(8,128)(2,1)} %shard_map.85), calls=%async_computation | async-start | bytes 2228224 | tf_op jit(solution)/shard_map/all_to_all | solution.py:292
  10.4 28.1 %copy-start = (bf16[1024,1024]{1,0:T(8,128)(2,1)S(1)}, bf16[1024,1024]{1,0:T(8,128)(2,1)}, u32[]{:S(2)}) copy-start(bf16[1024,1024]{1,0:T(8,128)(2,1)} %first_ref.1) | copy-start | bytes 6291460
  38.4 1.3 %copy-start.1 = (bf16[1024,512]{1,0:T(8,128)(2,1)S(1)}, bf16[1024,512]{1,0:T(8,128)(2,1)}, u32[]{:S(2)}) copy-start(bf16[1024,512]{1,0:T(8,128)(2,1)} %second_ref.3) | copy-start | bytes 3145732
  45.9 2.7 %collective-permute-start = (bf16[512,1024]{1,0:T(8,128)(2,1)S(1)}, bf16[512,1024]{1,0:T(8,128)(2,1)S(1)}, u32[]{:S(2)}, u32[]{:S(2)}) collective-permute-start(bf16[512,1024]{1,0:T(8,128)(2,1)S(1)} %get-tuple-element.47), channel_id=1, source_target_pairs={{0,1},{1,0},{2,3},{3,2},{4,5},{5,4},{6,7},{7,6},{8,9},{9,8},{10,11... | collective-permute-start | bytes 3145736 | tf_op jit(solution)/shard_map/ppermute | solution.py:255
  47.6 4.8 %collective-permute-start.6 = (bf16[512,512]{1,0:T(8,128)(2,1)S(1)}, bf16[512,512]{1,0:T(8,128)(2,1)S(1)}, u32[]{:S(2)}, u32[]{:S(2)}) collective-permute-start(bf16[512,512]{1,0:T(8,128)(2,1)S(1)} %get-tuple-element.59), channel_id=1, source_target_pairs={{0,1},{1,0},{2,3},{3,2},{4,5},{5,4},{6,7},{7,6},{8,9},{9,8},{10,11... | collective-permute-start | bytes 1572872 | tf_op jit(solution)/shard_map/ppermute | solution.py:255
  48.8 10.2 %collective-permute-start.1 = (bf16[4,32,1024]{2,1,0:T(8,128)(2,1)S(1)}, bf16[4,32,1024]{2,1,0:T(8,128)(2,1)S(1)}, u32[]{:S(2)}, u32[]{:S(2)}) collective-permute-start(bf16[4,32,1024]{2,1,0:T(8,128)(2,1)S(1)} %get-tuple-element.52), channel_id=1, source_target_pairs={{0,6},{1,7},{2,4},{3,5},{4,2},{5,3},{6,0},{7,1},{8,14},{9,15},{10,... | collective-permute-start | bytes 786440 | tf_op jit(solution)/shard_map/ppermute | solution.py:255
  51.2 12.5 %collective-permute-start.2 = (bf16[4,32,1024]{2,1,0:T(8,128)(2,1)S(1)}, bf16[4,32,1024]{2,1,0:T(8,128)(2,1)S(1)}, u32[]{:S(2)}, u32[]{:S(2)}) collective-permute-start(bf16[4,32,1024]{2,1,0:T(8,128)(2,1)S(1)} %get-tuple-element.53), channel_id=1, source_target_pairs={{0,2},{1,3},{2,0},{3,1},{4,6},{5,7},{6,4},{7,5},{8,10},{9,11},{10,... | collective-permute-start | bytes 786440 | tf_op jit(solution)/shard_map/ppermute | solution.py:255
  51.8 12.0 %collective-permute-start.3 = (bf16[4,32,1024]{2,1,0:T(8,128)(2,1)S(1)}, bf16[4,32,1024]{2,1,0:T(8,128)(2,1)S(1)}, u32[]{:S(2)}, u32[]{:S(2)}) collective-permute-start(bf16[4,32,1024]{2,1,0:T(8,128)(2,1)S(1)} %get-tuple-element.54), channel_id=1, source_target_pairs={{0,4},{1,5},{2,6},{3,7},{4,0},{5,1},{6,2},{7,3},{8,12},{9,13},{10,... | collective-permute-start | bytes 786440 | tf_op jit(solution)/shard_map/ppermute | solution.py:255
  52.4 13.6 %collective-permute-start.7 = (bf16[4,32,512]{2,1,0:T(8,128)(2,1)S(1)}, bf16[4,32,512]{2,1,0:T(8,128)(2,1)S(1)}, u32[]{:S(2)}, u32[]{:S(2)}) collective-permute-start(bf16[4,32,512]{2,1,0:T(8,128)(2,1)S(1)} %get-tuple-element.61), channel_id=1, source_target_pairs={{0,16},{8,24},{16,0},{24,8},{1,17},{9,25},{17,1},{25,9},{2,18},{10... | collective-permute-start | bytes 393224 | tf_op jit(solution)/shard_map/ppermute | solution.py:255
  53.7 14.7 %collective-permute-start.8 = (bf16[4,32,512]{2,1,0:T(8,128)(2,1)S(1)}, bf16[4,32,512]{2,1,0:T(8,128)(2,1)S(1)}, u32[]{:S(2)}, u32[]{:S(2)}) collective-permute-start(bf16[4,32,512]{2,1,0:T(8,128)(2,1)S(1)} %get-tuple-element.62), channel_id=1, source_target_pairs={{0,8},{8,0},{16,24},{24,16},{1,9},{9,1},{17,25},{25,17},{2,10},{10... | collective-permute-start | bytes 393224 | tf_op jit(solution)/shard_map/ppermute | solution.py:255
  58.9 9.4 %collective-permute-start.9 = (bf16[4,32,512]{2,1,0:T(8,128)(2,1)S(1)}, bf16[4,32,512]{2,1,0:T(8,128)(2,1)S(1)}, u32[]{:S(2)}, u32[]{:S(2)}) collective-permute-start(bf16[4,32,512]{2,1,0:T(8,128)(2,1)S(1)} %get-tuple-element.63), channel_id=1, source_target_pairs={{0,24},{8,16},{16,8},{24,0},{1,25},{9,17},{17,9},{25,1},{2,26},{10... | collective-permute-start | bytes 393224 | tf_op jit(solution)/shard_map/ppermute | solution.py:255
  63.9 5.0 %collective-permute-start.5 = (bf16[1,32,1024]{2,1,0:T(8,128)(2,1)S(1)}, bf16[1,32,1024]{2,1,0:T(8,128)(2,1)S(1)}, u32[]{:S(2)}, u32[]{:S(2)}) collective-permute-start(bf16[1,32,1024]{2,1,0:T(8,128)(2,1)S(1)} %get-tuple-element.57), channel_id=1, source_target_pairs={{0,8},{8,0},{16,24},{24,16},{1,9},{9,1},{17,25},{25,17},{2,10},{10... | collective-permute-start | bytes 196616 | tf_op jit(solution)/shard_map/ppermute | solution.py:255
  64.7 8.2 %collective-permute-start.4 = (bf16[1,32,1024]{2,1,0:T(8,128)(2,1)S(1)}, bf16[1,32,1024]{2,1,0:T(8,128)(2,1)S(1)}, u32[]{:S(2)}, u32[]{:S(2)}) collective-permute-start(bf16[1,32,1024]{2,1,0:T(8,128)(2,1)S(1)} %get-tuple-element.56), channel_id=1, source_target_pairs={{0,16},{8,24},{16,0},{24,8},{1,17},{9,25},{17,1},{25,9},{2,18},{10... | collective-permute-start | bytes 196616 | tf_op jit(solution)/shard_map/ppermute | solution.py:255
  66.0 6.9 %collective-permute-start.10 = (bf16[1,32,1024]{2,1,0:T(8,128)(2,1)S(1)}, bf16[1,32,1024]{2,1,0:T(8,128)(2,1)S(1)}, u32[]{:S(2)}, u32[]{:S(2)}) collective-permute-start(bf16[1,32,1024]{2,1,0:T(8,128)(2,1)S(1)} %get-tuple-element.69), channel_id=1, source_target_pairs={{0,24},{8,16},{16,8},{24,0},{1,25},{9,17},{17,9},{25,1},{2,26},{10... | collective-permute-start | bytes 196616 | tf_op jit(solution)/shard_map/ppermute | solution.py:255
  68.9 4.8 %collective-permute-start.11 = (bf16[1,32,512]{2,1,0:T(8,128)(2,1)S(1)}, bf16[1,32,512]{2,1,0:T(8,128)(2,1)S(1)}, u32[]{:S(2)}, u32[]{:S(2)}) collective-permute-start(bf16[1,32,512]{2,1,0:T(8,128)(2,1)S(1)} %get-tuple-element.71), channel_id=1, source_target_pairs={{0,6},{1,7},{2,4},{3,5},{4,2},{5,3},{6,0},{7,1},{8,14},{9,15},{10,... | collective-permute-start | bytes 98312 | tf_op jit(solution)/shard_map/ppermute | solution.py:255
  71.4 3.9 %collective-permute-start.12 = (bf16[1,32,512]{2,1,0:T(8,128)(2,1)S(1)}, bf16[1,32,512]{2,1,0:T(8,128)(2,1)S(1)}, u32[]{:S(2)}, u32[]{:S(2)}) collective-permute-start(bf16[1,32,512]{2,1,0:T(8,128)(2,1)S(1)} %get-tuple-element.72), channel_id=1, source_target_pairs={{0,2},{1,3},{2,0},{3,1},{4,6},{5,7},{6,4},{7,5},{8,10},{9,11},{10,... | collective-permute-start | bytes 98312 | tf_op jit(solution)/shard_map/ppermute | solution.py:255
  71.8 3.9 %collective-permute-start.13 = (bf16[1,32,512]{2,1,0:T(8,128)(2,1)S(1)}, bf16[1,32,512]{2,1,0:T(8,128)(2,1)S(1)}, u32[]{:S(2)}, u32[]{:S(2)}) collective-permute-start(bf16[1,32,512]{2,1,0:T(8,128)(2,1)S(1)} %get-tuple-element.73), channel_id=1, source_target_pairs={{0,4},{1,5},{2,6},{3,7},{4,0},{5,1},{6,2},{7,3},{8,12},{9,13},{10,... | collective-permute-start | bytes 98312 | tf_op jit(solution)/shard_map/ppermute | solution.py:255
